TPU v7x, 256 devices: a whole 4x4x8 slice. The times are simulated.
256 devices in a mesh: rows: 64 (over z, y, core), heads: 4 (over x).
Axes of the slice: x: 4, y: 4, z: 8, core: 2. Of those that a mesh axis runs over, the one named last changes fastest.
Arguments:
- row_layer_input: bfloat16 [256, 64, 768], P('rows'), may hold values from -6 to 6
- column_layer_input: bfloat16 [256, 64, 768], P('rows'), may hold values from -6 to 6
- feedforward_layer_input: bfloat16 [256, 64, 768], P('rows'), may hold values from -6 to 6
- grad_out: bfloat16 [256, 64, 768], P('rows'), may hold values from -16 to 16
- layer_norm_gains: float32 [3, 768], replicated, may hold values from 0.25 to 1.75
- row_qkv: bfloat16 [768, 3, 768], P(None, None, 'heads'), may hold values from -0.21875 to 0.21875
- row_out: bfloat16 [768, 768], P(None, 'heads'), may hold values from -0.21875 to 0.21875
- col_qkv: bfloat16 [768, 3, 768], P(None, None, 'heads'), may hold values from -0.21875 to 0.21875
- col_out: bfloat16 [768, 768], P(None, 'heads'), may hold values from -0.21875 to 0.21875
- ffn_up: bfloat16 [768, 3072], P(None, 'heads'), may hold values from -0.21875 to 0.21875
- ffn_down: bfloat16 [768, 3072], P(None, 'heads'), may hold values from -0.109375 to 0.109375
Outputs:
- input_gradient: bfloat16 [256, 64, 768], P('rows')
- grad_row_qkv: float32 [768, 3, 768], P('rows', None, 'heads')
- grad_row_out: float32 [768, 768], P('rows', 'heads')
- grad_col_qkv: float32 [768, 3, 768], P('rows', None, 'heads')
- grad_col_out: float32 [768, 768], P('rows', 'heads')
- grad_ffn_up: float32 [768, 3072], P('rows', 'heads')
- grad_ffn_down: float32 [768, 3072], P('rows', 'heads')
All inputs are finite; a program needn't handle non-finite values.
Results may differ from a plain program's by a relative error of at most 0.028.
Values may be sent and summed in bfloat16 or wider, within the bound.
No kernel may reach another device: no remote copies, remote signals or barrier semaphores. Data moves between devices by JAX's collectives and lax.ppermute only.
A program may use at most 128 MiB of HBM per device.

v0:
```python
import functools
import math

import jax
import jax.numpy as jnp
from jax import lax
from jax.experimental import pallas as pl
from jax.experimental.pallas import tpu as pltpu
from jax.sharding import PartitionSpec as P

DH = 64
eps = 1e-05
f32 = jnp.float32
bf16 = jnp.bfloat16


def pick(target, size):
    wide = lax.broadcasted_iota(jnp.int32, target.shape, 1)
    return jnp.where(wide == target, 1.0, 0.0).astype(f32).astype(bf16)


def row_index(rows, size):
    return lax.broadcasted_iota(jnp.int32, (rows, size), 0)


def column_from_natural(h, rows=256):
    u = row_index(rows, 256)
    return pick((u & 3) * 64 + (((u >> 2) + 16 * h) & 63), 256)


def row_from_natural(h):
    v = row_index(256, 256)
    return pick((v >> 6) * 64 + (((v & 63) + 16 * h) & 63), 256)


def column_from_row():
    u = row_index(256, 256)
    return pick((u & 3) * 64 + (u >> 2), 256)


def row_from_column():
    v = row_index(256, 256)
    return pick((v & 63) * 4 + (v >> 6), 256)


def natural_from_column(h):
    t = row_index(256, 256)
    return pick((((t & 63) - 16 * h) & 63) * 4 + (t >> 6), 256)


def dot(left, right):
    return lax.dot_general(left, right, (((1,), (0,)), ((), ())), preferred_element_type=f32)


def dot_tn(left, right):
    return lax.dot_general(left, right, (((0,), (0,)), ((), ())), preferred_element_type=f32)


def dot_nt(left, right):
    return lax.dot_general(left, right, (((1,), (1,)), ((), ())), preferred_element_type=f32)


def standardize(full):
    centered = full - jnp.mean(full, axis=-1, keepdims=True)
    inverse = lax.rsqrt(jnp.mean(centered * centered, axis=-1, keepdims=True) + eps)
    return centered * inverse, inverse


def softmax_rows(scores):
    top = jnp.max(scores, axis=-1, keepdims=True)
    expo = jnp.exp(scores - top)
    return expo / jnp.sum(expo, axis=-1, keepdims=True)


def softmax_back(probs, dprobs, scale):
    inner = jnp.sum(probs * dprobs, axis=-1, keepdims=True)
    return (probs * (dprobs - inner) * scale).astype(bf16)


def flat(ref):
    rows, cols, wide = ref.shape
    return ref[...].reshape(rows * cols, wide)


def feed_forward_kernel(
    h_ref, x_ref, go_ref, gain_ref, up_ref, down_ref,
    n_ref, gop_ref, act_ref, dpre_ref, xhat_ref, inv_ref, base_ref, d0, d1, d2, d3,
):
    order = column_from_natural(h_ref[0])
    xhat, inverse = standardize(dot(order, flat(x_ref)))
    normed = (xhat * gain_ref[2 : 3, :]).astype(bf16)
    n_ref[...] = normed
    send(n_ref)
    xhat_ref[...] = xhat[:64]
    inv_ref[...] = jnp.broadcast_to(inverse[:64], (64, 128))
    go = dot(order, flat(go_ref)).astype(bf16)
    gop_ref[...] = go
    base_ref[...] = go[:64]
    send(n_ref, gop_ref, xhat_ref, inv_ref)
    hpre = dot(normed, up_ref[...])
    half = 0.5 * (1.0 + lax.erf(hpre * (1.0 / math.sqrt(2.0))))
    act_ref[...] = (hpre * half).astype(bf16)
    slope = half + hpre * jnp.exp(-0.5 * hpre * hpre) * (1.0 / math.sqrt(2.0 * math.pi))
    dpre = (dot(go, down_ref[...]) * slope).astype(bf16)
    dpre_ref[...] = dpre
    send(act_ref, dpre_ref)
    dn = dot_nt(dpre, up_ref[...]).astype(bf16)
    for k, out in enumerate((d0, d1, d2, d3)):
        out[...] = dn[64 * k : 64 * (k + 1)]


def residual_kernel(
    base_ref, d0, d1, d2, d3, xhat_ref, inv_ref, gain_ref, full_ref, narrow_ref, *, norm
):
    dn = (
        (d0[...].astype(f32) + d1[...].astype(f32)) + d2[...].astype(f32)
    ) + d3[...].astype(f32)
    a = dn * gain_ref[norm : norm + 1, :]
    xhat = xhat_ref[...]
    first = jnp.mean(a, axis=-1, keepdims=True)
    second = jnp.mean(a * xhat, axis=-1, keepdims=True)
    g = base_ref[...].astype(f32) + inv_ref[:, :1] * (a - first - xhat * second)
    full_ref[...] = g
    narrow_ref[...] = g.astype(bf16)


def column_in_kernel(h_ref, x_ref, gain_ref, w_ref, n_ref, qkv_ref, xhat_ref, inv_ref):
    xhat, inverse = standardize(dot(column_from_natural(h_ref[0]), flat(x_ref)))
    normed = (xhat * gain_ref[1 : 2, :]).astype(bf16)
    n_ref[...] = normed
    send(n_ref)
    xhat_ref[...] = xhat[:64]
    inv_ref[...] = jnp.broadcast_to(inverse[:64], (64, 128))
    qkv_ref[...] = dot(normed, w_ref[...]).astype(bf16)


def row_in_kernel(
    h_ref, x_ref, gain_ref, w_ref, n_ref, qkv_ref, hi_lo_ref, xhat_ref, inv_ref, *, scale
):
    h = h_ref[0]
    x = flat(x_ref)
    xhat, _ = standardize(dot(row_from_natural(h), x))
    normed = (xhat * gain_ref[0 : 1, :]).astype(bf16)
    n_ref[...] = normed
    send(n_ref)
    own, inverse = standardize(dot(column_from_natural(h, 64), x))
    xhat_ref[...] = own
    inv_ref[...] = jnp.broadcast_to(inverse, (64, 128))
    qkv = dot(normed, w_ref[...]).astype(bf16)
    qkv_ref[...] = qkv
    local = qkv.shape[1] // 3
    parts = []
    for head in range(local // DH):
        total = jnp.zeros((64, 64), f32)
        for s in range(4):
            rows = slice(64 * s, 64 * (s + 1))
            q = qkv[rows, head * DH : (head + 1) * DH]
            k = qkv[rows, local + head * DH : local + (head + 1) * DH]
            total = total + dot_nt(q, k)
        parts.append(total * scale)
    parts.append(jnp.zeros((64, 64), f32))
    logits = jnp.concatenate(parts, axis=0)
    hi = logits.astype(bf16)
    lo = (logits - hi.astype(f32)).astype(bf16)
    order = column_from_row()
    hi_lo_ref[:, :DH] = dot(order, hi).astype(bf16)
    hi_lo_ref[:, DH:] = dot(order, lo).astype(bf16)


def column_out_kernel(g0, g1, g2, g3, w_ref, qkv_ref, hi_lo_ref, gz_ref, out_ref):
    for k, part in enumerate((g0, g1, g2, g3)):
        gz_ref[64 * k : 64 * (k + 1), :] = part[...]
    send(gz_ref)
    local = w_ref.shape[1]
    out_ref[:, : 3 * local] = qkv_ref[...]
    out_ref[:, 3 * local : 4 * local] = dot(gz_ref[...], w_ref[...]).astype(bf16)
    out_ref[:, 4 * local :] = hi_lo_ref[...]


def column_back_kernel(in_ref, out_ref, rprobs_ref):
    local = (in_ref.shape[1] - 2 * DH) // 4
    scale = 1.0 / math.sqrt(DH)
    for head in range(local // DH):
        at = head * DH
        q = in_ref[:, at : at + DH]
        k = in_ref[:, local + at : local + at + DH]
        v = in_ref[:, 2 * local + at : 2 * local + at + DH]
        og = in_ref[:, 3 * local + at : 3 * local + at + DH]
        probs = softmax_rows(dot_nt(q, k) * scale)
        narrow = probs.astype(bf16)
        ds = softmax_back(probs, dot_nt(og, v), scale)
        out_ref[:, at : at + DH] = dot(ds, k).astype(bf16)
        out_ref[:, local + at : local + at + DH] = dot_tn(ds, q).astype(bf16)
        out_ref[:, 2 * local + at : 2 * local + at + DH] = dot_tn(narrow, og).astype(bf16)
        out_ref[:, 3 * local + at : 3 * local + at + DH] = dot(narrow, v).astype(bf16)
    which = row_index(8, 256)
    source = lax.broadcasted_iota(jnp.int32, (8, 256), 1)
    total = jnp.where((source & 3) == which, 1.0, 0.0).astype(f32).astype(bf16)
    both = dot(total, in_ref[:, 4 * local : 4 * local + 2 * DH])
    probs = softmax_rows(both[:, :DH] + both[:, DH:])
    rprobs_ref[...] = probs
    spread = jnp.where((row_index(256, 8) & 3) == lax.broadcasted_iota(jnp.int32, (256, 8), 1), 1.0, 0.0)
    out_ref[:, 4 * local : 4 * local + DH] = dot(
        spread.astype(f32).astype(bf16), probs.astype(bf16)
    ).astype(bf16)


def column_join_kernel(back_ref, w_ref, d0, d1, d2, d3):
    local = w_ref.shape[1]
    dn = dot_nt(back_ref[:, :local], w_ref[...]).astype(bf16)
    for k, out in enumerate((d0, d1, d2, d3)):
        out[...] = dn[64 * k : 64 * (k + 1)]


def tied_probs(back_ref, local):
    return dot(row_from_column(), back_ref[:, 4 * local : 4 * local + DH]).astype(bf16)


def row_out_kernel(g0, g1, g2, g3, w_ref, qkv_ref, gy_ref, og_ref, dprobs_ref):
    gy = jnp.concatenate([g0[...], g1[...], g2[...], g3[...]], axis=0)
    gy = dot(row_from_column(), gy).astype(bf16)
    gy_ref[...] = gy
    send(gy_ref)
    og = dot(gy, w_ref[...]).astype(bf16)
    og_ref[...] = og
    send(og_ref)
    local = og.shape[1]
    parts = []
    for head in range(local // DH):
        at = head * DH
        total = jnp.zeros((64, 64), f32)
        for s in range(4):
            rows = slice(64 * s, 64 * (s + 1))
            v = qkv_ref[rows, 2 * local + at : 2 * local + at + DH]
            total = total + dot_nt(og[rows, at : at + DH], v)
        parts.append(total)
    whole = jnp.concatenate(parts, axis=1)
    for row in range(64):
        dprobs_ref[row] = whole[row : row + 1, :]


def row_values_kernel(back_ref, qkv_ref, og_ref, att_ref, dv_ref):
    local = og_ref.shape[1]
    probs = tied_probs(back_ref, local)
    for head in range(local // DH):
        at = head * DH
        p = probs[64 * head : 64 * (head + 1)]
        for s in range(4):
            rows = slice(64 * s, 64 * (s + 1))
            v = qkv_ref[rows, 2 * local + at : 2 * local + at + DH]
            att_ref[rows, at : at + DH] = dot(p, v).astype(bf16)
            dv_ref[rows, at : at + DH] = dot_tn(p, og_ref[rows, at : at + DH]).astype(bf16)


def tied_back_kernel(got_ref, probs_ref, out_ref, *, scale):
    total = jnp.sum(got_ref[...], axis=0)
    parts = []
    for head in range(total.shape[1] // DH):
        at = head * DH
        ds = softmax_back(probs_ref[head : head + 1, :], total[:, at : at + DH], scale)
        parts.append(ds.astype(f32))
    whole = jnp.concatenate(parts, axis=1)
    out_ref[...] = jnp.broadcast_to(whole.reshape(1, *whole.shape), out_ref.shape)


def row_join_kernel(dl_ref, qkv_ref, dv_ref, w_ref, dq_ref, dk_ref, d0, d1, d2, d3, dl_all):
    local = dv_ref.shape[1]
    for row in range(64):
        dl_all[row : row + 1, :] = dl_ref[row]
    for head in range(local // DH):
        at = head * DH
        dl = dl_all[:, at : at + DH].astype(bf16)
        for s in range(4):
            rows = slice(64 * s, 64 * (s + 1))
            q = qkv_ref[rows, at : at + DH]
            k = qkv_ref[rows, local + at : local + at + DH]
            dq_ref[rows, at : at + DH] = dot(dl, k).astype(bf16)
            dk_ref[rows, at : at + DH] = dot_tn(dl, q).astype(bf16)
    dn = (
        dot_nt(dq_ref[...], w_ref[:, :local])
        + dot_nt(dk_ref[...], w_ref[:, local : 2 * local])
        + dot_nt(dv_ref[...], w_ref[:, 2 * local :])
    ).astype(bf16)
    dn = dot(column_from_row(), dn).astype(bf16)
    for k, out in enumerate((d0, d1, d2, d3)):
        out[...] = dn[64 * k : 64 * (k + 1)]


def natural_kernel(h_ref, g0, g1, g2, g3, out_ref):
    g = jnp.concatenate([g0[...], g1[...], g2[...], g3[...]], axis=0)
    g = dot(natural_from_column(h_ref[0]), g).astype(bf16)
    out_ref[...] = g.reshape(out_ref.shape)


def packed(parts, row, share):
    tiles = [
        part[share * row : share * (row + 1), at : at + 128]
        for part in parts
        for at in range(0, part.shape[1], 128)
    ]
    return jnp.concatenate(tiles, axis=0)


def scatter_order(parts, out_ref, devices=64, zs=8):
    share = parts[0].shape[0] // devices
    size = out_ref.shape[0] // devices
    for row in range(devices):
        at = size * ((row % (devices // zs)) * zs + row // (devices // zs))
        out_ref[at : at + size, :] = packed(parts, row, share)


def ffn_weight_kernel(n_ref, dpre_ref, go_ref, act_ref, out_ref):
    parts = [dot_tn(n_ref[...], dpre_ref[...]), dot_tn(go_ref[...], act_ref[...])]
    scatter_order(parts, out_ref)


def split_cores(at_ref, whole, keep_ref, send_ref):
    share = whole.shape[0] // (2 * keep_ref.shape[0])
    first = at_ref[0] == 0
    for chip in range(keep_ref.shape[0]):
        low, high = [packed([whole], row, share) for row in (2 * chip, 2 * chip + 1)]
        keep_ref[chip] = jnp.where(first, low, high).astype(bf16)
        send_ref[chip] = jnp.where(first, high, low).astype(bf16)


def column_weight_kernel(at_ref, n_ref, back_ref, gz_ref, keep_ref, send_ref, *, local):
    whole = jnp.concatenate(
        [
            dot_tn(n_ref[...], back_ref[:, : 3 * local]),
            dot_tn(gz_ref[...], back_ref[:, 3 * local : 4 * local]),
        ],
        axis=1,
    )
    split_cores(at_ref, whole, keep_ref, send_ref)


def row_weight_kernel(at_ref, n_ref, dq_ref, dk_ref, dv_ref, gy_ref, att_ref, keep_ref, send_ref):
    normed = n_ref[...]
    whole = jnp.concatenate(
        [
            dot_tn(normed, dq_ref[...]),
            dot_tn(normed, dk_ref[...]),
            dot_tn(normed, dv_ref[...]),
            dot_tn(gy_ref[...], att_ref[...]),
        ],
        axis=1,
    )
    split_cores(at_ref, whole, keep_ref, send_ref)


def pair_kernel(keep_a, got_a, keep_b, got_b, out_ref):
    size = keep_a.shape[1]
    out_ref[:, :size] = (keep_a[...].astype(f32) + got_a[...].astype(f32)).astype(bf16)
    out_ref[:, size:] = (keep_b[...].astype(f32) + got_b[...].astype(f32)).astype(bf16)


def unpacked(tiles, share):
    return jnp.concatenate(
        [tiles[at : at + share] for at in range(0, tiles.shape[0], share)], axis=1
    )


def ffn_end_kernel(got_ref, up_ref, down_ref):
    share, wide = up_ref.shape
    whole = unpacked(got_ref[...], share)
    up_ref[...] = whole[:, :wide]
    down_ref[...] = whole[:, wide:]


def attention_end_kernel(got_ref, qkv_a, out_a, qkv_b, out_b):
    total = jnp.sum(got_ref[...].astype(f32), axis=0)
    share, local = out_a.shape
    half = total.shape[0] // 2
    for tiles, qkv_ref, out_ref in (
        (total[:half], qkv_a, out_a),
        (total[half:], qkv_b, out_b),
    ):
        whole = unpacked(tiles, share)
        for k in range(3):
            qkv_ref[:, k, :] = whole[:, local * k : local * (k + 1)]
        out_ref[...] = whole[:, 3 * local :]


def after(x, *first):
    return lax.optimization_barrier((x, *first))[0]


def shaped(*shape, kind=bf16):
    return jax.ShapeDtypeStruct(shape, kind)


class Fetched:
    def __init__(self, source, buffer, sem):
        self.buffer = buffer
        self.shape = buffer.shape
        self.copy = pltpu.make_async_copy(source, buffer, sem)
        self.copy.start()
        self.waiting = True

    def ready(self):
        if self.waiting:
            self.copy.wait()
            self.waiting = False

    def __getitem__(self, at):
        self.ready()
        return self.buffer[at]


class Kept:
    def __init__(self, buffer, target, sem):
        self.buffer = buffer
        self.shape = buffer.shape
        self.dtype = buffer.dtype
        self.copy = pltpu.make_async_copy(buffer, target, sem)
        self.sent = False

    def __setitem__(self, at, value):
        self.buffer[at] = value

    def __getitem__(self, at):
        return self.buffer[at]

    def send(self):
        if not self.sent:
            self.copy.start()
            self.sent = True


def send(*refs):
    for ref in refs:
        if isinstance(ref, Kept):
            ref.send()


def call(body, outs, *args, near=(), near_outs=(), scratch=(), small=False, **options):
    kinds = [
        "scalar" if a.dtype == jnp.int32 else "near" if i in near else "far"
        for i, a in enumerate(args)
    ]
    out_kinds = ["near" if i in near_outs else "far" for i in range(len(outs))]
    far = [a for a, kind in zip(args, kinds) if kind == "far"]
    far_outs = [o for o, kind in zip(outs, out_kinds) if kind == "far"]
    space = {"scalar": pltpu.SMEM, "near": pltpu.VMEM, "far": pltpu.HBM}

    def kernel(*refs):
        ins, refs = refs[: len(args)], refs[len(args) :]
        results, refs = refs[: len(outs)], refs[len(outs) :]
        own, refs = refs[: len(scratch)], refs[len(scratch) :]
        buffers, sems = list(refs[:-1]), refs[-1]
        fetched, given = [], []
        for ref, kind in zip(ins, kinds):
            if kind == "far":
                fetched.append(Fetched(ref, buffers[len(fetched)], sems.at[len(fetched)]))
                given.append(fetched[-1])
            else:
                given.append(ref)
        stores = []
        for ref, kind in zip(results, out_kinds):
            if kind == "far":
                k = len(fetched) + len(stores)
                stores.append(Kept(buffers[k], ref, sems.at[k]))
                given.append(stores[-1])
            else:
                given.append(ref)
        body(*given, *own, **options)
        for one in fetched:
            one.ready()
        send(*stores)
        for store in stores:
            store.copy.wait()

    moved = sum(math.prod(a.shape) * a.dtype.itemsize for a in (*args, *outs))
    return pl.pallas_call(
        kernel,
        out_shape=[
            pltpu.HBM(o.shape, o.dtype) if kind == "far" else o
            for o, kind in zip(outs, out_kinds)
        ],
        in_specs=[pl.BlockSpec(memory_space=space[kind]) for kind in kinds],
        out_specs=[pl.BlockSpec(memory_space=space[kind]) for kind in out_kinds],
        scratch_shapes=list(scratch)
        + [pltpu.VMEM(a.shape, a.dtype) for a in (*far, *far_outs)]
        + [pltpu.SemaphoreType.DMA((max(len(far) + len(far_outs), 1),))],
        compiler_params=pltpu.CompilerParams(vmem_limit_bytes=28 * 1024 * 1024),
        cost_estimate=pl.CostEstimate(
            flops=1000 if small else 3 * 10**9,
            bytes_accessed=1000 if small else 30 * moved,
            transcendentals=0,
        ),
        name=body.__name__,
    )(
        *(
            pltpu.with_memory_space_constraint(a, pltpu.HBM) if kind == "far" else a
            for a, kind in zip(args, kinds)
        )
    )


class Moves:
    def __init__(self, mesh):
        self.heads = mesh.shape["heads"]
        self.rows = mesh.shape["rows"]
        self.ys = 4
        self.zs = self.rows // (2 * self.ys)
        self.z_groups = [
            [z * 2 * self.ys + rest for z in range(self.zs)] for rest in range(2 * self.ys)
        ]
        each = 2 * self.ys
        self.slice_groups = [
            list(range(each * z, each * (z + 1))) for z in range(self.zs)
        ]
        self.core_groups = [list(range(core, self.rows, 2)) for core in range(2)]
        self.pair = [(i, i ^ 1) for i in range(self.rows)]

    def shift_heads(self, x, k):
        n = self.heads
        return lax.ppermute(x, "heads", [(i, (i + k) % n) for i in range(n)])

    def scatter_heads(self, parts):
        return [parts[0]] + [self.shift_heads(parts[k], k) for k in range(1, self.heads)]

    def gather_heads(self, own):
        return [own] + [self.shift_heads(own, -k) for k in range(1, self.heads)]

    def all_to_all(self, x, groups=None):
        return lax.all_to_all(
            x, "rows", split_axis=0, concat_axis=0, tiled=True, axis_index_groups=groups
        )

    def messages(self, x):
        wide = x.shape[1]
        got = self.all_to_all(x.reshape(self.rows, x.shape[0] // self.rows, wide))
        return got.reshape(x.shape[0], wide)

    def swap(self, x):
        return lax.ppermute(x, "rows", self.pair)

    def sum_rows(self, x):
        for groups in (self.slice_groups, self.z_groups):
            x = lax.psum_scatter(
                x, "rows", scatter_dimension=0, tiled=True, axis_index_groups=groups
            )
        return x


def solution(mesh):
    moves = Moves(mesh)

    def per_device(
        row_layer_input,
        column_layer_input,
        feedforward_layer_input,
        grad_out,
        layer_norm_gains,
        row_qkv,
        row_out,
        col_qkv,
        col_out,
        ffn_up,
        ffn_down,
    ):
        seqs, cols, width = row_layer_input.shape
        tokens = seqs * cols
        hidden = ffn_up.shape[1]
        local = col_out.shape[1]
        own = tokens // moves.heads
        h = lax.axis_index("heads").reshape(1)
        index = lax.axis_index("rows")
        core = index % 2
        at = jnp.stack([core, (index // 2) % moves.ys])
        gains = layer_norm_gains
        col_flat = col_qkv.reshape(width, 3 * local)
        row_flat = row_qkv.reshape(width, 3 * local)
        row_scale = 1.0 / math.sqrt(DH * seqs * moves.rows)
        whole, piece = shaped(tokens, width), shaped(own, width)
        piece_full, column = shaped(own, width, kind=f32), shaped(own, 128, kind=f32)
        heads_out = shaped(tokens, local)
        triple = shaped(tokens, 3 * local)

        n2, gop, act, dpre, xhat2, inv2, base, *parts2 = call(
            feed_forward_kernel,
            [whole, whole, shaped(tokens, hidden), shaped(tokens, hidden), piece_full, column]
            + [piece] * 5,
            h, feedforward_layer_input, grad_out, gains, ffn_up, ffn_down, near_outs=(6, 7, 8, 9, 10),
        )
        parts2 = moves.scatter_heads(parts2)
        ffn_shape = shaped(width * 2 * hidden // 128, 128, kind=f32)
        (g_ffn,) = call(
            ffn_weight_kernel, [ffn_shape], after(n2, *parts2), dpre, gop, act, small=True
        )
        ffn_got = moves.sum_rows(g_ffn)
        gz_own, gz_narrow = call(
            residual_kernel, [piece_full, piece], base, *parts2, xhat2, inv2, gains, near=(0, 1, 2, 3, 4), near_outs=(1,), norm=2
        )
        gz_parts = moves.gather_heads(gz_narrow)
        n1, col_all, xhat1, inv1 = call(
            column_in_kernel, [whole, triple, piece_full, column],
            after(h, n2), column_layer_input, gains, col_flat, near=(3,),
        )
        n0, row_all, hi_lo, xhat0, inv0 = call(
            row_in_kernel,
            [whole, triple, shaped(tokens, 2 * DH), piece_full, column],
            after(h, n2), row_layer_input, gains, row_flat, near=(3,), scale=row_scale,
        )

        gz, col_in = call(
            column_out_kernel,
            [whole, shaped(tokens, 4 * local + 2 * DH)],
            *gz_parts, col_out, col_all, after(hi_lo, g_ffn), near=(0, 1, 2, 3), near_outs=(1,),
        )
        col_in = moves.messages(col_in)
        back, rprobs = call(
            column_back_kernel,
            [shaped(tokens, 4 * local + DH), shaped(8, DH, kind=f32)],
            col_in, near=(0,), near_outs=(0,),
        )
        back = moves.messages(back)
        parts1 = call(
            column_join_kernel, [piece] * 4, back, col_flat, near=(0, 1), near_outs=(0, 1, 2, 3)
        )
        parts1 = moves.scatter_heads(parts1)
        gy_own, gy_narrow = call(
            residual_kernel, [piece_full, piece], gz_own, *parts1, xhat1, inv1, gains, near=(1, 2, 3, 4), near_outs=(1,), norm=1
        )
        gy_parts = moves.gather_heads(gy_narrow)
        share = width // moves.rows
        piece_rows = share * 4 * local // 128
        cores = shaped(moves.rows // 2, piece_rows, 128)
        col_keep, col_send = call(
            column_weight_kernel, [cores, cores], at, after(n1, gy_narrow), back, gz,
            small=True, local=local,
        )

        gy, row_og, dprobs = call(
            row_out_kernel,
            [whole, heads_out, shaped(cols, 1, local, kind=f32)],
            *gy_parts, row_out, row_all, near=(0, 1, 2, 3), near_outs=(2,),
        )
        got = moves.all_to_all(dprobs)
        col_got = moves.swap(after(col_send, dprobs))
        row_att, row_dv = call(
            row_values_kernel, [heads_out, heads_out], back, row_all, after(row_og, dprobs),
            small=True,
        )
        (dl,) = call(
            tied_back_kernel, [shaped(cols, 1, local, kind=f32)], got, rprobs, near=(0,), near_outs=(0,), scale=row_scale
        )
        dl = after(moves.all_to_all(dl), ffn_got)
        row_dq, row_dk, *parts0 = call(
            row_join_kernel, [heads_out] * 2 + [piece] * 4,
            dl, row_all, row_dv, row_flat,
            near=(0, 3), near_outs=(0, 1, 2, 3, 4, 5),
            scratch=[pltpu.VMEM((cols, local), f32)],
        )
        parts0 = moves.scatter_heads(parts0)
        row_keep, row_send = call(
            row_weight_kernel, [cores, cores],
            at, n0, row_dq, row_dk, row_dv, gy, row_att, near=(2, 3), near_outs=(0, 1),
        )
        (late,) = call(
            pair_kernel, [shaped(moves.rows // 2, 2 * piece_rows, 128)],
            col_keep, col_got, row_keep, moves.swap(row_send), near=(2, 3), near_outs=(0,),
        )
        late = moves.all_to_all(late, moves.core_groups)
        _, gx_narrow = call(
            residual_kernel, [piece_full, piece], gy_own, *parts0, xhat0, inv0, gains, near=(1, 2, 3, 4), near_outs=(1,), norm=0
        )
        gx_parts = moves.gather_heads(gx_narrow)
        (input_gradient,) = call(
            natural_kernel, [shaped(seqs, cols, width)], h, *gx_parts, near=(1, 2, 3, 4)
        )
        qkv_share = shaped(share, 3, local, kind=f32)
        out_share = shaped(share, local, kind=f32)
        ffn_share = shaped(share, hidden, kind=f32)
        g_up, g_down = call(ffn_end_kernel, [ffn_share, ffn_share], ffn_got)
        g_cqkv, g_cout, g_rqkv, g_rout = call(
            attention_end_kernel, [qkv_share, out_share] * 2, late, near=(0,)
        )
        return (input_gradient, g_rqkv, g_rout, g_cqkv, g_cout, g_up, g_down)

    return jax.shard_map(
        per_device,
        mesh=mesh,
        in_specs=(
            P("rows", None, None),
            P("rows", None, None),
            P("rows", None, None),
            P("rows", None, None),
            P(),
            P(None, None, "heads"),
            P(None, "heads"),
            P(None, None, "heads"),
            P(None, "heads"),
            P(None, "heads"),
            P(None, "heads"),
        ),
        out_specs=(
            P("rows", None, None),
            P("rows", None, "heads"),
            P("rows", "heads"),
            P("rows", None, "heads"),
            P("rows", "heads"),
            P("rows", "heads"),
            P("rows", "heads"),
        ),
        check_vma=False,
    )
```

profile of v0, /device:TPU:32, one launch (start us, length us, event | category | flops | bytes accessed | tf_op | source)
XLA Modules:
  0.0 206.5 jit_solution(9421872183024609094)
XLA Ops:
  7.2 4.0 %feed_forward_kernel.1 = (bf16[256,768]{1,0:T(8,128)(2,1)}, bf16[256,768]{1,0:T(8,128)(2,1)}, bf16[256,768]{1,0:T(8,128)(2,1)}, bf16[256,768]{1,0:T(8,128)(2,1)}...) custom-call(s32[1]{0:T(128)} %bitcast.refs_0_, ...), custom_call_target="tpu_custom_call" | custom-call | flops 3000000000 | bytes 163461248 | tf_op jit(solution)/shard_map/feed_forward_kernel/pallas_call | solution.py:474
  11.2 1.6 collective-permute-start
  12.8 2.7 %collective-permute-start.1 = (bf16[64,768]{1,0:T(8,128)(2,1)S(1)}, bf16[64,768]{1,0:T(8,128)(2,1)S(1)}, u32[]{:S(2)}, u32[]{:S(2)}) collective-permute-start(bf16[64,768]{1,0:T(8,128)(2,1)S(1)} %get-tuple-element.71), channel_id=1, source_target_pairs={{0,2},{1,3},{2,0},{3,1},{4,6},{5,7},{6,4},{7,5},{8,10},{9,11},{10,... | collective-permute-start | bytes 294920 | tf_op jit(solution)/shard_map/ppermute | solution.py:518
  15.5 1.4 collective-permute-start.2
  16.9 0.4 collective-permute-done.refs_2_
  17.3 2.8 %collective-permute-done.1.refs_3_ = bf16[64,768]{1,0:T(8,128)(2,1)S(1)} collective-permute-done((bf16[64,768]{1,0:T(8,128)(2,1)S(1)}, bf16[64,768]{1,0:T(8,128)(2,1)S(1)}, u32[]{:S(2)}, u32[]{:S(2)}) %collective-permute-start.1) | collective-permute-done | bytes 98336 | tf_op jit(solution)/shard_map/ppermute | solution.py:518
  20.1 4.6 %ffn_weight_kernel.1 = f32[9216,128]{1,0:T(8,128)} custom-call(bf16[256,768]{1,0:T(8,128)(2,1)} %get-tuple-element.81.refs_0_, bf16[256,768]{1,0:T(8,128)(2,1)} %get-tuple-element.82.refs_1_, bf16[256,768]{1,0:T(8,128)(2,1)} %get-tuple-element.83.refs_2_, bf16[256,768]{1,0:T(8,128)(2,1)} %get-tuple-element.84.refs_3_), custom_call_target="tpu_custom_call" | custom-call | flops 1000 | bytes 1000 | tf_op jit(solution)/shard_map/ffn_weight_kernel/pallas_call | solution.py:474
  24.8 1.1 copy-done.1
  25.9 0.6 copy.23.refs_3_
  26.6 0.6 copy.22.refs_3_.refs_1_
  27.2 3.3 %row_in_kernel.1 = (bf16[256,768]{1,0:T(8,128)(2,1)}, bf16[256,576]{1,0:T(8,128)(2,1)}, bf16[256,128]{1,0:T(8,128)(2,1)}, f32[64,768]{1,0:T(8,128)}, f32[64,128]{1,0:T(8,128)}) custom-call(s32[1]{0:T(128)} %bitcast.refs_0_, bf16[4,64,768]{2,1,0:T(8,128)(2,1)} %refs_1_.5, f32[3,768]{1,0:T(4,128)} %refs_7_.5, bf16[768,576]{1,0:T(8,128)(2,1)S(1)} %copy.23.refs_3_), custom_call_target="tpu_custom_call" | custom-call | flops 3000000000 | bytes 68106360 | tf_op jit(solution)/shard_map/row_in_kernel/pallas_call | solution.py:474
  30.5 1.9 residual_kernel.3
  32.4 2.7 %collective-permute-start.3 = (bf16[64,768]{1,0:T(8,128)(2,1)S(1)}, bf16[64,768]{1,0:T(8,128)(2,1)S(1)}, u32[]{:S(2)}, u32[]{:S(2)}) collective-permute-start(bf16[64,768]{1,0:T(8,128)(2,1)S(1)} %get-tuple-element.76.refs_0_), channel_id=1, source_target_pairs={{0,3},{1,0},{2,1},{3,2},{4,7},{5,4},{6,5},{7,6},{8,11},{9,8},{10,9... | collective-permute-start | bytes 294920 | tf_op jit(solution)/shard_map/ppermute | solution.py:518
  35.1 0.8 collective-permute-start.4
  35.9 0.7 collective-permute-start.5
  36.5 2.9 %column_in_kernel.1 = (bf16[256,768]{1,0:T(8,128)(2,1)}, bf16[256,576]{1,0:T(8,128)(2,1)}, f32[64,768]{1,0:T(8,128)}, f32[64,128]{1,0:T(8,128)}) custom-call(s32[1]{0:T(128)} %bitcast.refs_0_, bf16[4,64,768]{2,1,0:T(8,128)(2,1)} %refs_1_.4, f32[3,768]{1,0:T(4,128)} %refs_7_.5, bf16[768,576]{1,0:T(8,128)(2,1)S(1)} %copy.22.refs_3_.refs_1_), custom_call_target="tpu_custom_call" | custom-call | flops 3000000000 | bytes 66140280 | tf_op jit(solution)/shard_map/column_in_kernel/pallas_call | solution.py:474
  39.4 0.9 copy.24.refs_4_
  40.4 0.9 collective-permute-done.4.refs_2_
  41.3 1.0 collective-permute-done.5.refs_3_
  42.3 1.7 column_out_kernel.1
  44.1 27.0 %all_to_all.25 = bf16[64,4,896]{2,1,0:T(4,128)(2,1)S(1)} all-to-all(bf16[64,4,896]{2,1,0:T(4,128)(2,1)S(1)} %reshape.38), channel_id=1, replica_groups=mesh['rows'=64,'heads'=4] {'rows'}, dimensions={0} | all-to-all | bytes 917504 | tf_op jit(solution)/shard_map/all_to_all | solution.py:527
  71.2 2.8 %column_back_kernel.1 = (bf16[256,832]{1,0:T(8,128)(2,1)S(1)}, f32[8,64]{1,0:T(8,128)}) custom-call(bf16[256,896]{1,0:T(8,128)(2,1)S(1)} %reshape.39.refs_0_), custom_call_target="tpu_custom_call" | custom-call | flops 3000000000 | bytes 26603520 | tf_op jit(solution)/shard_map/column_back_kernel/pallas_call | solution.py:474
  74.1 21.8 %all_to_all.26 = bf16[64,4,832]{2,1,0:T(4,128)(2,1)S(1)} all-to-all(bf16[64,4,832]{2,1,0:T(4,128)(2,1)S(1)} %reshape.40), channel_id=1, replica_groups=mesh['rows'=64,'heads'=4] {'rows'}, dimensions={0} | all-to-all | bytes 851968 | tf_op jit(solution)/shard_map/all_to_all | solution.py:527
  96.2 0.5 column_join_kernel.1
  96.7 0.3 copy-done
  97.2 2.0 collective-permute-start.7
  99.2 1.4 collective-permute-start.8
  100.6 4.8 %collective-permute-done.6.refs_2_ = bf16[64,768]{1,0:T(8,128)(2,1)S(1)} collective-permute-done((bf16[64,768]{1,0:T(8,128)(2,1)S(1)}, bf16[64,768]{1,0:T(8,128)(2,1)S(1)}, u32[]{:S(2)}, u32[]{:S(2)}) %collective-permute-start.6) | collective-permute-done | bytes 98336 | tf_op jit(solution)/shard_map/ppermute | solution.py:518
  105.4 0.6 collective-permute-done.8.refs_4_
  106.0 2.0 residual_kernel.4
  108.1 1.0 collective-permute-start.10
  109.1 2.4 %collective-permute-start.11 = (bf16[64,768]{1,0:T(8,128)(2,1)S(1)}, bf16[64,768]{1,0:T(8,128)(2,1)S(1)}, u32[]{:S(2)}, u32[]{:S(2)}) collective-permute-start(bf16[64,768]{1,0:T(8,128)(2,1)S(1)} %get-tuple-element.95.refs_0_), channel_id=1, source_target_pairs={{0,1},{1,2},{2,3},{3,0},{4,5},{5,6},{6,7},{7,4},{8,9},{9,10},{10,1... | collective-permute-start | bytes 294920 | tf_op jit(solution)/shard_map/ppermute | solution.py:518
  111.4 0.9 collective-permute-start.9
  112.3 0.9 copy.26.refs_4_
  113.3 1.5 collective-permute-done.10.refs_2_
  114.8 1.0 collective-permute-done.11.refs_3_
  115.8 0.4 collective-permute-done.9.refs_1_
  116.1 2.7 %row_out_kernel.1 = (bf16[256,768]{1,0:T(8,128)(2,1)}, bf16[256,192]{1,0:T(8,128)(2,1)}, f32[64,1,192]{2,1,0:T(1,128)}) custom-call(bf16[64,768]{1,0:T(8,128)(2,1)S(1)} %get-tuple-element.95.refs_0_, bf16[64,768]{1,0:T(8,128)(2,1)S(1)} %collective-permute-done.9.refs_1_, bf16[64,768]{1,0:T(8,128)(2,1)S(1)} %collective-permute-done.10.refs_2_, ...), custom_call_target="tpu_custom_call" | custom-call | flops 3000000000 | bytes 45711360 | tf_op jit(solution)/shard_map/row_out_kernel/pallas_call | solution.py:474
  118.9 6.0 %all-to-all-start.2 = ((f32[64,1,192]{2,1,0:T(1,128)}), f32[64,1,192]{2,1,0:T(1,128)S(1)}, u32[]{:S(2)}, u32[]{:S(2)}) async-start(f32[64,1,192]{2,1,0:T(1,128)} %get-tuple-element.97), calls=%async_computation.2 | async-start | bytes 131072 | tf_op jit(solution)/shard_map/all_to_all | solution.py:527
  124.9 9.0 %all-to-all-done.2.refs_0_ = f32[64,1,192]{2,1,0:T(1,128)S(1)} async-done(((f32[64,1,192]{2,1,0:T(1,128)}), f32[64,1,192]{2,1,0:T(1,128)S(1)}, u32[]{:S(2)}, u32[]{:S(2)}) %all-to-all-start.2) | async-done | bytes 49184 | tf_op jit(solution)/shard_map/all_to_all | solution.py:527
  133.9 1.6 tied_back_kernel.1
  135.6 6.2 %all-to-all-start.3 = ((f32[64,1,192]{2,1,0:T(1,128)}), f32[64,1,192]{2,1,0:T(1,128)S(1)}, u32[]{:S(2)}, u32[]{:S(2)}) async-start(f32[64,1,192]{2,1,0:T(1,128)} %tied_back_kernel.1), calls=%async_computation.3 | async-start | bytes 131072 | tf_op jit(solution)/shard_map/all_to_all | solution.py:527
  141.8 3.9 %column_weight_kernel.1 = (bf16[32,72,128]{2,1,0:T(8,128)(2,1)}, bf16[32,72,128]{2,1,0:T(8,128)(2,1)}) custom-call(s32[2]{0:T(128)S(1)} %pad_add_fusion.refs_0_, bf16[256,768]{1,0:T(8,128)(2,1)} %get-tuple-element.111.refs_1_, bf16[256,832]{1,0:T(8,128)(2,1)} %copy-done, bf16[256,768]{1,0:T(8,128)(2,1)} %get-tuple-element.112.refs_3_), custom_call_target="tpu_custom_call" | custom-call | flops 1000 | bytes 1000 | tf_op jit(solution)/shard_map/column_weight_kernel/pallas_call | solution.py:474
  145.7 2.4 %row_values_kernel.1 = (bf16[256,192]{1,0:T(8,128)(2,1)}, bf16[256,192]{1,0:T(8,128)(2,1)}) custom-call(bf16[256,832]{1,0:T(8,128)(2,1)} %copy-done, bf16[256,576]{1,0:T(8,128)(2,1)} %get-tuple-element.96.refs_5_.refs_1_, bf16[256,192]{1,0:T(8,128)(2,1)} %get-tuple-element.101.refs_2_), custom_call_target="tpu_custom_call" | custom-call | flops 1000 | bytes 1000 | tf_op jit(solution)/shard_map/row_values_kernel/pallas_call | solution.py:474
  148.4 2.5 %all-to-all-done.3.refs_0_ = f32[64,1,192]{2,1,0:T(1,128)S(1)} async-done(((f32[64,1,192]{2,1,0:T(1,128)}), f32[64,1,192]{2,1,0:T(1,128)S(1)}, u32[]{:S(2)}, u32[]{:S(2)}) %all-to-all-start.3) | async-done | bytes 49184 | tf_op jit(solution)/shard_map/all_to_all | solution.py:527
  150.9 2.2 %row_join_kernel.1 = (bf16[256,192]{1,0:T(8,128)(2,1)S(1)}, bf16[256,192]{1,0:T(8,128)(2,1)S(1)}, bf16[64,768]{1,0:T(8,128)(2,1)S(1)}, bf16[64,768]{1,0:T(8,128)...) custom-call(f32[64,1,192]{2,1,0:T(1,128)S(1)} %all-to-all-done.3.refs_0_, ...), custom_call_target="tpu_custom_call" | custom-call | flops 3000000000 | bytes 57507840 | tf_op jit(solution)/shard_map/row_join_kernel/pallas_call | solution.py:474
  153.2 2.9 %row_weight_kernel.1 = (bf16[32,72,128]{2,1,0:T(8,128)(2,1)S(1)}, bf16[32,72,128]{2,1,0:T(8,128)(2,1)S(1)}) custom-call(s32[2]{0:T(128)S(1)} %pad_add_fusion.refs_0_, bf16[256,768]{1,0:T(8,128)(2,1)} %get-tuple-element.116.refs_1_, bf16[256,192]{1,0:T(8,128)(2,1)S(1)} %get-tuple-element.117.refs_2_, bf16[256,192]{1,0:T(8,128)(2,1)S(1)} %get-tuple-element.118.refs_3_, ...), custom_call_target="tpu_custom_call" | custom-call | flops 3000000000 | bytes 70779120 | tf_op jit(solution)/shard_map/row_weight_kernel/pallas_call | solution.py:474
  156.3 1.9 collective-permute-done.19.refs_3_
  158.1 2.5 %pair_kernel.1 = bf16[32,144,128]{2,1,0:T(8,128)(2,1)} custom-call(bf16[32,72,128]{2,1,0:T(8,128)(2,1)} %get-tuple-element.113.refs_0_, bf16[32,72,128]{2,1,0:T(8,128)(2,1)} %copy-done.5, bf16[32,72,128]{2,1,0:T(8,128)(2,1)S(1)} %get-tuple-element.121.refs_2_, bf16[32,72,128]{2,1,0:T(8,128)(2,1)S(1)} %collective-permute-done.19.refs_3_), custom_call_target="tpu_custom_call" | custom-call | flops 3000000000 | bytes 106168320 | tf_op jit(solution)/shard_map/pair_kernel/pallas_call | solution.py:474
  160.7 7.5 %all-to-all-start.4 = ((bf16[32,144,128]{2,1,0:T(8,128)(2,1)}), bf16[32,144,128]{2,1,0:T(8,128)(2,1)S(1)}, u32[]{:S(2)}, u32[]{:S(2)}) async-start(bf16[32,144,128]{2,1,0:T(8,128)(2,1)} %pair_kernel.1), calls=%async_computation.6 | async-start | bytes 2359296 | tf_op jit(solution)/shard_map/all_to_all | solution.py:527
  168.2 0.5 collective-permute-start.12
  168.7 3.5 %collective-permute-start.13 = (bf16[64,768]{1,0:T(8,128)(2,1)S(1)}, bf16[64,768]{1,0:T(8,128)(2,1)S(1)}, u32[]{:S(2)}, u32[]{:S(2)}) collective-permute-start(bf16[64,768]{1,0:T(8,128)(2,1)S(1)} %get-tuple-element.105), channel_id=1, source_target_pairs={{0,2},{1,3},{2,0},{3,1},{4,6},{5,7},{6,4},{7,5},{8,10},{9,11},{10,... | collective-permute-start | bytes 294920 | tf_op jit(solution)/shard_map/ppermute | solution.py:518
  172.2 2.5 %collective-permute-done.12.refs_2_ = bf16[64,768]{1,0:T(8,128)(2,1)S(1)} collective-permute-done((bf16[64,768]{1,0:T(8,128)(2,1)S(1)}, bf16[64,768]{1,0:T(8,128)(2,1)S(1)}, u32[]{:S(2)}, u32[]{:S(2)}) %collective-permute-start.12) | collective-permute-done | bytes 98336 | tf_op jit(solution)/shard_map/ppermute | solution.py:518
  174.7 2.1 %collective-permute-done.13.refs_3_ = bf16[64,768]{1,0:T(8,128)(2,1)S(1)} collective-permute-done((bf16[64,768]{1,0:T(8,128)(2,1)S(1)}, bf16[64,768]{1,0:T(8,128)(2,1)S(1)}, u32[]{:S(2)}, u32[]{:S(2)}) %collective-permute-start.13) | collective-permute-done | bytes 98336 | tf_op jit(solution)/shard_map/ppermute | solution.py:518
  177.0 1.9 residual_kernel.5
  179.0 2.3 %collective-permute-start.15 = (bf16[64,768]{1,0:T(8,128)(2,1)S(1)}, bf16[64,768]{1,0:T(8,128)(2,1)S(1)}, u32[]{:S(2)}, u32[]{:S(2)}) collective-permute-start(bf16[64,768]{1,0:T(8,128)(2,1)S(1)} %get-tuple-element.109.refs_1_), channel_id=1, source_target_pairs={{0,3},{1,0},{2,1},{3,2},{4,7},{5,4},{6,5},{7,6},{8,11},{9,8},{10,9... | collective-permute-start | bytes 294920 | tf_op jit(solution)/shard_map/ppermute | solution.py:518
  181.4 0.9 collective-permute-start.17
  182.3 1.5 ffn_end_kernel.1
  183.9 1.3 collective-permute-done.15.refs_2_
  185.2 2.7 %collective-permute-done.16.refs_3_ = bf16[64,768]{1,0:T(8,128)(2,1)S(1)} collective-permute-done((bf16[64,768]{1,0:T(8,128)(2,1)S(1)}, bf16[64,768]{1,0:T(8,128)(2,1)S(1)}, u32[]{:S(2)}, u32[]{:S(2)}) %collective-permute-start.16) | collective-permute-done | bytes 98336 | tf_op jit(solution)/shard_map/ppermute | solution.py:518
  187.9 0.7 collective-permute-done.17.refs_4_
  188.6 1.0 natural_kernel.1
  189.6 9.1 %all-to-all-done.4.refs_0_ = bf16[32,144,128]{2,1,0:T(8,128)(2,1)S(1)} async-done(((bf16[32,144,128]{2,1,0:T(8,128)(2,1)}), bf16[32,144,128]{2,1,0:T(8,128)(2,1)S(1)}, u32[]{:S(2)}, u32[]{:S(2)}) %all-to-all-start.4) | async-done | bytes 1179680 | tf_op jit(solution)/shard_map/all_to_all | solution.py:527
  198.7 1.0 attention_end_kernel.1
  (31 shorter events, 1.8 us)
Async XLA Ops:
  7.2 93.4 %reduce-scatter.3.cloned.1.call-start = ((), (), s32[]{:S(2)}) async-start(), calls=%async_computation.7 | async-start | bytes 5308416 | tf_op jit(solution)/shard_map/reduce_scatter | solution.py:541
  11.2 6.1 %collective-permute-start = (bf16[64,768]{1,0:T(8,128)(2,1)S(1)}, bf16[64,768]{1,0:T(8,128)(2,1)S(1)}, u32[]{:S(2)}, u32[]{:S(2)}) collective-permute-start(bf16[64,768]{1,0:T(8,128)(2,1)S(1)} %get-tuple-element.70), channel_id=1, source_target_pairs={{0,1},{1,2},{2,3},{3,0},{4,5},{5,6},{6,7},{7,4},{8,9},{9,10},{10,1... | collective-permute-start | bytes 294920 | tf_op jit(solution)/shard_map/ppermute | solution.py:518
  12.8 7.3 %collective-permute-start.1 = (bf16[64,768]{1,0:T(8,128)(2,1)S(1)}, bf16[64,768]{1,0:T(8,128)(2,1)S(1)}, u32[]{:S(2)}, u32[]{:S(2)}) collective-permute-start(bf16[64,768]{1,0:T(8,128)(2,1)S(1)} %get-tuple-element.71), channel_id=1, source_target_pairs={{0,2},{1,3},{2,0},{3,1},{4,6},{5,7},{6,4},{7,5},{8,10},{9,11},{10,... | collective-permute-start | bytes 294920 | tf_op jit(solution)/shard_map/ppermute | solution.py:518
  15.5 4.6 %collective-permute-start.2 = (bf16[64,768]{1,0:T(8,128)(2,1)S(1)}, bf16[64,768]{1,0:T(8,128)(2,1)S(1)}, u32[]{:S(2)}, u32[]{:S(2)}) collective-permute-start(bf16[64,768]{1,0:T(8,128)(2,1)S(1)} %get-tuple-element.72), channel_id=1, source_target_pairs={{0,3},{1,0},{2,1},{3,2},{4,7},{5,4},{6,5},{7,6},{8,11},{9,8},{10,9... | collective-permute-start | bytes 294920 | tf_op jit(solution)/shard_map/ppermute | solution.py:518
  24.7 1.2 copy-start.1
  24.8 1.8 copy-start.2
  24.8 126.2 %reduce-scatter.5.cloned.1.call-start = ((), (), s32[]{:S(2)}) async-start(), calls=%async_computation.8 | async-start | bytes 663552 | tf_op jit(solution)/shard_map/reduce_scatter | solution.py:541
  32.4 7.1 %copy-start.3 = (bf16[768,192]{0,1:T(8,128)(2,1)S(1)}, bf16[768,192]{0,1:T(8,128)(2,1)}, u32[]{:S(2)}) copy-start(bf16[768,192]{0,1:T(8,128)(2,1)} %param.19) | copy-start | bytes 884740
  32.4 8.0 %collective-permute-start.3 = (bf16[64,768]{1,0:T(8,128)(2,1)S(1)}, bf16[64,768]{1,0:T(8,128)(2,1)S(1)}, u32[]{:S(2)}, u32[]{:S(2)}) collective-permute-start(bf16[64,768]{1,0:T(8,128)(2,1)S(1)} %get-tuple-element.76.refs_0_), channel_id=1, source_target_pairs={{0,3},{1,0},{2,1},{3,2},{4,7},{5,4},{6,5},{7,6},{8,11},{9,8},{10,9... | collective-permute-start | bytes 294920 | tf_op jit(solution)/shard_map/ppermute | solution.py:518
  35.1 6.2 %collective-permute-start.4 = (bf16[64,768]{1,0:T(8,128)(2,1)S(1)}, bf16[64,768]{1,0:T(8,128)(2,1)S(1)}, u32[]{:S(2)}, u32[]{:S(2)}) collective-permute-start(bf16[64,768]{1,0:T(8,128)(2,1)S(1)} %get-tuple-element.76.refs_0_), channel_id=1, source_target_pairs={{0,2},{1,3},{2,0},{3,1},{4,6},{5,7},{6,4},{7,5},{8,10},{9,11},{10,... | collective-permute-start | bytes 294920 | tf_op jit(solution)/shard_map/ppermute | solution.py:518
  35.9 6.4 %collective-permute-start.5 = (bf16[64,768]{1,0:T(8,128)(2,1)S(1)}, bf16[64,768]{1,0:T(8,128)(2,1)S(1)}, u32[]{:S(2)}, u32[]{:S(2)}) collective-permute-start(bf16[64,768]{1,0:T(8,128)(2,1)S(1)} %get-tuple-element.76.refs_0_), channel_id=1, source_target_pairs={{0,1},{1,2},{2,3},{3,0},{4,5},{5,6},{6,7},{7,4},{8,9},{9,10},{10,1... | collective-permute-start | bytes 294920 | tf_op jit(solution)/shard_map/ppermute | solution.py:518
  96.2 0.8 copy-start
  97.0 8.4 %collective-permute-start.6 = (bf16[64,768]{1,0:T(8,128)(2,1)S(1)}, bf16[64,768]{1,0:T(8,128)(2,1)S(1)}, u32[]{:S(2)}, u32[]{:S(2)}) collective-permute-start(bf16[64,768]{1,0:T(8,128)(2,1)S(1)} %get-tuple-element.89), channel_id=1, source_target_pairs={{0,1},{1,2},{2,3},{3,0},{4,5},{5,6},{6,7},{7,4},{8,9},{9,10},{10,1... | collective-permute-start | bytes 294920 | tf_op jit(solution)/shard_map/ppermute | solution.py:518
  97.2 8.2 %collective-permute-start.7 = (bf16[64,768]{1,0:T(8,128)(2,1)S(1)}, bf16[64,768]{1,0:T(8,128)(2,1)S(1)}, u32[]{:S(2)}, u32[]{:S(2)}) collective-permute-start(bf16[64,768]{1,0:T(8,128)(2,1)S(1)} %get-tuple-element.90), channel_id=1, source_target_pairs={{0,2},{1,3},{2,0},{3,1},{4,6},{5,7},{6,4},{7,5},{8,10},{9,11},{10,... | collective-permute-start | bytes 294920 | tf_op jit(solution)/shard_map/ppermute | solution.py:518
  99.2 6.9 %collective-permute-start.8 = (bf16[64,768]{1,0:T(8,128)(2,1)S(1)}, bf16[64,768]{1,0:T(8,128)(2,1)S(1)}, u32[]{:S(2)}, u32[]{:S(2)}) collective-permute-start(bf16[64,768]{1,0:T(8,128)(2,1)S(1)} %get-tuple-element.91), channel_id=1, source_target_pairs={{0,3},{1,0},{2,1},{3,2},{4,7},{5,4},{6,5},{7,6},{8,11},{9,8},{10,9... | collective-permute-start | bytes 294920 | tf_op jit(solution)/shard_map/ppermute | solution.py:518
  106.0 6.3 %copy-start.4 = (bf16[768,192]{0,1:T(8,128)(2,1)S(1)}, bf16[768,192]{0,1:T(8,128)(2,1)}, u32[]{:S(2)}) copy-start(bf16[768,192]{0,1:T(8,128)(2,1)} %param.17) | copy-start | bytes 884740
  108.1 6.7 %collective-permute-start.10 = (bf16[64,768]{1,0:T(8,128)(2,1)S(1)}, bf16[64,768]{1,0:T(8,128)(2,1)S(1)}, u32[]{:S(2)}, u32[]{:S(2)}) collective-permute-start(bf16[64,768]{1,0:T(8,128)(2,1)S(1)} %get-tuple-element.95.refs_0_), channel_id=1, source_target_pairs={{0,2},{1,3},{2,0},{3,1},{4,6},{5,7},{6,4},{7,5},{8,10},{9,11},{10,... | collective-permute-start | bytes 294920 | tf_op jit(solution)/shard_map/ppermute | solution.py:518
  109.1 6.7 %collective-permute-start.11 = (bf16[64,768]{1,0:T(8,128)(2,1)S(1)}, bf16[64,768]{1,0:T(8,128)(2,1)S(1)}, u32[]{:S(2)}, u32[]{:S(2)}) collective-permute-start(bf16[64,768]{1,0:T(8,128)(2,1)S(1)} %get-tuple-element.95.refs_0_), channel_id=1, source_target_pairs={{0,1},{1,2},{2,3},{3,0},{4,5},{5,6},{6,7},{7,4},{8,9},{9,10},{10,1... | collective-permute-start | bytes 294920 | tf_op jit(solution)/shard_map/ppermute | solution.py:518
  111.4 4.7 %collective-permute-start.9 = (bf16[64,768]{1,0:T(8,128)(2,1)S(1)}, bf16[64,768]{1,0:T(8,128)(2,1)S(1)}, u32[]{:S(2)}, u32[]{:S(2)}) collective-permute-start(bf16[64,768]{1,0:T(8,128)(2,1)S(1)} %get-tuple-element.95.refs_0_), channel_id=1, source_target_pairs={{0,3},{1,0},{2,1},{3,2},{4,7},{5,4},{6,5},{7,6},{8,11},{9,8},{10,9... | collective-permute-start | bytes 294920 | tf_op jit(solution)/shard_map/ppermute | solution.py:518
  118.9 15.0 %all-to-all-start.2 = ((f32[64,1,192]{2,1,0:T(1,128)}), f32[64,1,192]{2,1,0:T(1,128)S(1)}, u32[]{:S(2)}, u32[]{:S(2)}) async-start(f32[64,1,192]{2,1,0:T(1,128)} %get-tuple-element.97), calls=%async_computation.2 | async-start | bytes 131072 | tf_op jit(solution)/shard_map/all_to_all | solution.py:527
  135.6 15.4 %all-to-all-start.3 = ((f32[64,1,192]{2,1,0:T(1,128)}), f32[64,1,192]{2,1,0:T(1,128)S(1)}, u32[]{:S(2)}, u32[]{:S(2)}) async-start(f32[64,1,192]{2,1,0:T(1,128)} %tied_back_kernel.1), calls=%async_computation.3 | async-start | bytes 131072 | tf_op jit(solution)/shard_map/all_to_all | solution.py:527
  148.2 8.1 %collective-permute-start.18 = (bf16[32,72,128]{2,1,0:T(8,128)(2,1)}, bf16[32,72,128]{2,1,0:T(8,128)(2,1)S(1)}, u32[]{:S(2)}, u32[]{:S(2)}) collective-permute-start(bf16[32,72,128]{2,1,0:T(8,128)(2,1)} %get-tuple-element.115), channel_id=1, source_target_pairs={{0,4},{4,0},{8,12},{12,8},{16,20},{20,16},{24,28},{28,24},{32,36},... | collective-permute-start | bytes 1769480 | tf_op jit(solution)/shard_map/ppermute | solution.py:537
  156.0 2.1 %collective-permute-start.19 = (bf16[32,72,128]{2,1,0:T(8,128)(2,1)S(1)}, bf16[32,72,128]{2,1,0:T(8,128)(2,1)S(1)}, u32[]{:S(2)}, u32[]{:S(2)}) collective-permute-start(bf16[32,72,128]{2,1,0:T(8,128)(2,1)S(1)} %get-tuple-element.122), channel_id=1, source_target_pairs={{0,4},{4,0},{8,12},{12,8},{16,20},{20,16},{24,28},{28,24},{32,36},... | collective-permute-start | bytes 1769480 | tf_op jit(solution)/shard_map/ppermute | solution.py:537
  156.3 1.9 copy-start.5
  160.7 38.0 %all-to-all-start.4 = ((bf16[32,144,128]{2,1,0:T(8,128)(2,1)}), bf16[32,144,128]{2,1,0:T(8,128)(2,1)S(1)}, u32[]{:S(2)}, u32[]{:S(2)}) async-start(bf16[32,144,128]{2,1,0:T(8,128)(2,1)} %pair_kernel.1), calls=%async_computation.6 | async-start | bytes 2359296 | tf_op jit(solution)/shard_map/all_to_all | solution.py:527
  168.2 6.5 %collective-permute-start.12 = (bf16[64,768]{1,0:T(8,128)(2,1)S(1)}, bf16[64,768]{1,0:T(8,128)(2,1)S(1)}, u32[]{:S(2)}, u32[]{:S(2)}) collective-permute-start(bf16[64,768]{1,0:T(8,128)(2,1)S(1)} %get-tuple-element.104), channel_id=1, source_target_pairs={{0,1},{1,2},{2,3},{3,0},{4,5},{5,6},{6,7},{7,4},{8,9},{9,10},{10,1... | collective-permute-start | bytes 294920 | tf_op jit(solution)/shard_map/ppermute | solution.py:518
  168.7 8.1 %collective-permute-start.13 = (bf16[64,768]{1,0:T(8,128)(2,1)S(1)}, bf16[64,768]{1,0:T(8,128)(2,1)S(1)}, u32[]{:S(2)}, u32[]{:S(2)}) collective-permute-start(bf16[64,768]{1,0:T(8,128)(2,1)S(1)} %get-tuple-element.105), channel_id=1, source_target_pairs={{0,2},{1,3},{2,0},{3,1},{4,6},{5,7},{6,4},{7,5},{8,10},{9,11},{10,... | collective-permute-start | bytes 294920 | tf_op jit(solution)/shard_map/ppermute | solution.py:518
  172.2 4.8 %collective-permute-start.14 = (bf16[64,768]{1,0:T(8,128)(2,1)S(1)}, bf16[64,768]{1,0:T(8,128)(2,1)S(1)}, u32[]{:S(2)}, u32[]{:S(2)}) collective-permute-start(bf16[64,768]{1,0:T(8,128)(2,1)S(1)} %get-tuple-element.106), channel_id=1, source_target_pairs={{0,3},{1,0},{2,1},{3,2},{4,7},{5,4},{6,5},{7,6},{8,11},{9,8},{10,9... | collective-permute-start | bytes 294920 | tf_op jit(solution)/shard_map/ppermute | solution.py:518
  179.0 6.2 %collective-permute-start.15 = (bf16[64,768]{1,0:T(8,128)(2,1)S(1)}, bf16[64,768]{1,0:T(8,128)(2,1)S(1)}, u32[]{:S(2)}, u32[]{:S(2)}) collective-permute-start(bf16[64,768]{1,0:T(8,128)(2,1)S(1)} %get-tuple-element.109.refs_1_), channel_id=1, source_target_pairs={{0,3},{1,0},{2,1},{3,2},{4,7},{5,4},{6,5},{7,6},{8,11},{9,8},{10,9... | collective-permute-start | bytes 294920 | tf_op jit(solution)/shard_map/ppermute | solution.py:518
  181.3 6.6 %collective-permute-start.16 = (bf16[64,768]{1,0:T(8,128)(2,1)S(1)}, bf16[64,768]{1,0:T(8,128)(2,1)S(1)}, u32[]{:S(2)}, u32[]{:S(2)}) collective-permute-start(bf16[64,768]{1,0:T(8,128)(2,1)S(1)} %get-tuple-element.109.refs_1_), channel_id=1, source_target_pairs={{0,2},{1,3},{2,0},{3,1},{4,6},{5,7},{6,4},{7,5},{8,10},{9,11},{10,... | collective-permute-start | bytes 294920 | tf_op jit(solution)/shard_map/ppermute | solution.py:518
  181.4 7.2 %collective-permute-start.17 = (bf16[64,768]{1,0:T(8,128)(2,1)S(1)}, bf16[64,768]{1,0:T(8,128)(2,1)S(1)}, u32[]{:S(2)}, u32[]{:S(2)}) collective-permute-start(bf16[64,768]{1,0:T(8,128)(2,1)S(1)} %get-tuple-element.109.refs_1_), channel_id=1, source_target_pairs={{0,1},{1,2},{2,3},{3,0},{4,5},{5,6},{6,7},{7,4},{8,9},{9,10},{10,1... | collective-permute-start | bytes 294920 | tf_op jit(solution)/shard_map/ppermute | solution.py:518
Sparse Core Ops, SparseCore 0:
  24.9 47.0 reduce-scatter.2
  100.7 33.9 reduce-scatter.4
where the time goes:
time: 208 us; the launch traced here: 206 us
  blocking collectives  48.8 us (23%)
  Pallas kernels  47.5 us (23%)
  waiting for transfers between devices  45.4 us (22%)
  starting transfers between devices  45.3 us (22%)
  between operations  14.4 us (7%)
  local copies, waits for them, and re-layouts  5.01 us (2%)
    all_to_all x2, blocking collectives, all_to_all(): lax.all_to_all(x, 'rows', split_axis=0, concat_axis=0, tiled=True, axis_i...  48.8 us
    pallas_call x20, Pallas kernels, call(): pl.pallas_call(kernel, out_shape=[pltpu.HBM(o.shape, o.dtype) if kind ==...  47.5 us
    ppermute x18, starting transfers between devices, shift_heads(): return lax.ppermute(x, 'heads', [(i, (i + k) % n) for i in range(n)])  25.1 us
    ppermute x18, waiting for transfers between devices, shift_heads(): return lax.ppermute(x, 'heads', [(i, (i + k) % n) for i in range(n)])  23 us
    all_to_all x3, waiting for transfers between devices, all_to_all(): lax.all_to_all(x, 'rows', split_axis=0, concat_axis=0, tiled=True, axis_i...  20.6 us
    all_to_all x3, starting transfers between devices, all_to_all(): lax.all_to_all(x, 'rows', split_axis=0, concat_axis=0, tiled=True, axis_i...  19.6 us
  transfers between devices with their start and end apart: 25, of which 19 were waited for; matrix products, arithmetic and copies ran while one was open for 2% of the time, Pallas kernels for 17%

commit v1 on v0

--- a/solution.py
+++ b/solution.py
@@ -148,6 +148,7 @@
     inv_ref[...] = jnp.broadcast_to(inverse, (64, 128))
     qkv = dot(normed, w_ref[...]).astype(bf16)
     qkv_ref[...] = qkv
+    send(qkv_ref, xhat_ref, inv_ref)
     local = qkv.shape[1] // 3
     parts = []
     for head in range(local // DH):
@@ -165,6 +166,19 @@
     order = column_from_row()
     hi_lo_ref[:, :DH] = dot(order, hi).astype(bf16)
     hi_lo_ref[:, DH:] = dot(order, lo).astype(bf16)
+
+
+def inputs_kernel(
+    h_ref, x1_ref, x0_ref, gain_ref, w1_ref, w0_ref,
+    n1_ref, qkv1_ref, xhat1_ref, inv1_ref,
+    n0_ref, qkv0_ref, hi_lo_ref, xhat0_ref, inv0_ref, *, scale,
+):
+    column_in_kernel(h_ref, x1_ref, gain_ref, w1_ref, n1_ref, qkv1_ref, xhat1_ref, inv1_ref)
+    send(qkv1_ref, xhat1_ref, inv1_ref)
+    row_in_kernel(
+        h_ref, x0_ref, gain_ref, w0_ref,
+        n0_ref, qkv0_ref, hi_lo_ref, xhat0_ref, inv0_ref, scale=scale,
+    )
 
 
 def column_out_kernel(g0, g1, g2, g3, w_ref, qkv_ref, hi_lo_ref, gz_ref, out_ref):
@@ -350,8 +364,16 @@
 
 def pair_kernel(keep_a, got_a, keep_b, got_b, out_ref):
     size = keep_a.shape[1]
+    out_ref[:, size:] = (keep_b[...].astype(f32) + got_b[...].astype(f32)).astype(bf16)
     out_ref[:, :size] = (keep_a[...].astype(f32) + got_a[...].astype(f32)).astype(bf16)
-    out_ref[:, size:] = (keep_b[...].astype(f32) + got_b[...].astype(f32)).astype(bf16)
+
+
+def row_end_kernel(
+    at_ref, dl_ref, w_ref, qkv_ref, dv_ref, n_ref, gy_ref, att_ref,
+    d0, d1, d2, d3, keep_ref, send_ref, dl_all, dq, dk,
+):
+    row_join_kernel(dl_ref, qkv_ref, dv_ref, w_ref, dq, dk, d0, d1, d2, d3, dl_all)
+    row_weight_kernel(at_ref, n_ref, dq, dk, dv_ref, gy_ref, att_ref, keep_ref, send_ref)
 
 
 def unpacked(tiles, share):
@@ -587,22 +609,22 @@
         parts2 = moves.scatter_heads(parts2)
         ffn_shape = shaped(width * 2 * hidden // 128, 128, kind=f32)
         (g_ffn,) = call(
-            ffn_weight_kernel, [ffn_shape], after(n2, *parts2), dpre, gop, act, small=True
-        )
-        ffn_got = moves.sum_rows(g_ffn)
+            ffn_weight_kernel, [ffn_shape], n2, dpre, gop, act, small=True
+        )
         gz_own, gz_narrow = call(
             residual_kernel, [piece_full, piece], base, *parts2, xhat2, inv2, gains, near=(0, 1, 2, 3, 4), near_outs=(1,), norm=2
         )
         gz_parts = moves.gather_heads(gz_narrow)
-        n1, col_all, xhat1, inv1 = call(
-            column_in_kernel, [whole, triple, piece_full, column],
-            after(h, n2), column_layer_input, gains, col_flat, near=(3,),
-        )
-        n0, row_all, hi_lo, xhat0, inv0 = call(
-            row_in_kernel,
-            [whole, triple, shaped(tokens, 2 * DH), piece_full, column],
-            after(h, n2), row_layer_input, gains, row_flat, near=(3,), scale=row_scale,
-        )
+        (
+            n1, col_all, xhat1, inv1, n0, row_all, hi_lo, xhat0, inv0
+        ) = call(
+            inputs_kernel,
+            [whole, triple, piece_full, column]
+            + [whole, triple, shaped(tokens, 2 * DH), piece_full, column],
+            after(h, gz_narrow), column_layer_input, row_layer_input, gains, col_flat, row_flat,
+            near=(4, 5), scale=row_scale,
+        )
+        ffn_got = moves.sum_rows(g_ffn)
 
         gz, col_in = call(
             column_out_kernel,
@@ -613,7 +635,7 @@
         back, rprobs = call(
             column_back_kernel,
             [shaped(tokens, 4 * local + DH), shaped(8, DH, kind=f32)],
-            col_in, near=(0,), near_outs=(0,),
+            col_in, near=(0,), near_outs=(0, 1),
         )
         back = moves.messages(back)
         parts1 = call(
@@ -644,20 +666,16 @@
             small=True,
         )
         (dl,) = call(
-            tied_back_kernel, [shaped(cols, 1, local, kind=f32)], got, rprobs, near=(0,), near_outs=(0,), scale=row_scale
+            tied_back_kernel, [shaped(cols, 1, local, kind=f32)], got, rprobs, near=(0, 1), near_outs=(0,), scale=row_scale
         )
         dl = after(moves.all_to_all(dl), ffn_got)
-        row_dq, row_dk, *parts0 = call(
-            row_join_kernel, [heads_out] * 2 + [piece] * 4,
-            dl, row_all, row_dv, row_flat,
-            near=(0, 3), near_outs=(0, 1, 2, 3, 4, 5),
-            scratch=[pltpu.VMEM((cols, local), f32)],
+        *parts0, row_keep, row_send = call(
+            row_end_kernel, [piece] * 4 + [cores, cores],
+            at, dl, row_flat, row_all, row_dv, n0, gy, row_att,
+            near=(1, 2), near_outs=(0, 1, 2, 3, 4, 5),
+            scratch=[pltpu.VMEM((cols, local), f32)] + [pltpu.VMEM((tokens, local), bf16)] * 2,
         )
         parts0 = moves.scatter_heads(parts0)
-        row_keep, row_send = call(
-            row_weight_kernel, [cores, cores],
-            at, n0, row_dq, row_dk, row_dv, gy, row_att, near=(2, 3), near_outs=(0, 1),
-        )
         (late,) = call(
             pair_kernel, [shaped(moves.rows // 2, 2 * piece_rows, 128)],
             col_keep, col_got, row_keep, moves.swap(row_send), near=(2, 3), near_outs=(0,),

time: 208 us -> 200 us (0.962)
  Pallas kernels: 47.5 us -> 43.1 us
  waiting for transfers between devices: 45.4 us -> 41.7 us
    pallas_call x20 -> x18, Pallas kernels: 47.5 us -> 43.1 us  [call(): pl.pallas_call(kernel, out_shape=[pltpu.HBM(o.shape, o.dtype) if kind ==...]
    ppermute x18, waiting for transfers between devices: 23 us -> 19.4 us  [shift_heads(): return lax.ppermute(x, 'heads', [(i, (i + k) % n) for i in range(n)])]
  transfers between devices with their start and end apart: 25 -> 25, of which waited for: 19 -> 17; matrix products, arithmetic and copies ran while one was open for 2% -> 2% of each run, Pallas kernels for 17% -> 16%
where the time goes in v1:
time: 200 us; the launch traced here: 199 us
  blocking collectives  48.8 us (24%)
  starting transfers between devices  45.7 us (23%)
  Pallas kernels  43.1 us (22%)
  waiting for transfers between devices  41.7 us (21%)
  between operations  14.4 us (7%)
  local copies, waits for them, and re-layouts  4.86 us (2%)
    all_to_all x2, blocking collectives, all_to_all(): lax.all_to_all(x, 'rows', split_axis=0, concat_axis=0, tiled=True, axis_i...  48.8 us
    pallas_call x18, Pallas kernels, call(): pl.pallas_call(kernel, out_shape=[pltpu.HBM(o.shape, o.dtype) if kind ==...  43.1 us
    ppermute x18, starting transfers between devices, shift_heads(): return lax.ppermute(x, 'heads', [(i, (i + k) % n) for i in range(n)])  25.1 us
    all_to_all x3, waiting for transfers between devices, all_to_all(): lax.all_to_all(x, 'rows', split_axis=0, concat_axis=0, tiled=True, axis_i...  20.4 us
    all_to_all x3, starting transfers between devices, all_to_all(): lax.all_to_all(x, 'rows', split_axis=0, concat_axis=0, tiled=True, axis_i...  19.8 us
    ppermute x18, waiting for transfers between devices, shift_heads(): return lax.ppermute(x, 'heads', [(i, (i + k) % n) for i in range(n)])  19.4 us
  transfers between devices with their start and end apart: 25, of which 17 were waited for; matrix products, arithmetic and copies ran while one was open for 2% of the time, Pallas kernels for 16%

profile of v1, /device:TPU:32, one launch (start us, length us, event | category | flops | bytes accessed | tf_op | source)
XLA Modules:
  0.0 198.6 jit_solution(8182980618153195416)
XLA Ops:
  7.2 4.0 %feed_forward_kernel.1 = (bf16[256,768]{1,0:T(8,128)(2,1)}, bf16[256,768]{1,0:T(8,128)(2,1)}, bf16[256,768]{1,0:T(8,128)(2,1)}, bf16[256,768]{1,0:T(8,128)(2,1)}...) custom-call(s32[1]{0:T(128)} %bitcast.refs_0_, ...), custom_call_target="tpu_custom_call" | custom-call | flops 3000000000 | bytes 163461248 | tf_op jit(solution)/shard_map/feed_forward_kernel/pallas_call | solution.py:496
  11.2 4.6 %ffn_weight_kernel.1 = f32[9216,128]{1,0:T(8,128)} custom-call(bf16[256,768]{1,0:T(8,128)(2,1)} %get-tuple-element.77.refs_0_, bf16[256,768]{1,0:T(8,128)(2,1)} %get-tuple-element.78.refs_1_, bf16[256,768]{1,0:T(8,128)(2,1)} %get-tuple-element.79.refs_2_, bf16[256,768]{1,0:T(8,128)(2,1)} %get-tuple-element.80.refs_3_), custom_call_target="tpu_custom_call" | custom-call | flops 1000 | bytes 1000 | tf_op jit(solution)/shard_map/ffn_weight_kernel/pallas_call | solution.py:496
  15.9 1.6 collective-permute-start
  17.5 2.7 %collective-permute-start.1 = (bf16[64,768]{1,0:T(8,128)(2,1)S(1)}, bf16[64,768]{1,0:T(8,128)(2,1)S(1)}, u32[]{:S(2)}, u32[]{:S(2)}) collective-permute-start(bf16[64,768]{1,0:T(8,128)(2,1)S(1)} %get-tuple-element.68), channel_id=1, source_target_pairs={{0,2},{1,3},{2,0},{3,1},{4,6},{5,7},{6,4},{7,5},{8,10},{9,11},{10,... | collective-permute-start | bytes 294920 | tf_op jit(solution)/shard_map/ppermute | solution.py:540
  20.2 1.4 collective-permute-start.2
  21.7 0.6 copy.22.refs_4_.refs_1_
  22.3 1.6 copy.23.refs_5_.refs_2_
  23.9 0.9 copy.24.refs_4_
  24.8 1.9 residual_kernel.3
  26.7 2.7 %collective-permute-start.3 = (bf16[64,768]{1,0:T(8,128)(2,1)S(1)}, bf16[64,768]{1,0:T(8,128)(2,1)S(1)}, u32[]{:S(2)}, u32[]{:S(2)}) collective-permute-start(bf16[64,768]{1,0:T(8,128)(2,1)S(1)} %get-tuple-element.73.refs_0_), channel_id=1, source_target_pairs={{0,3},{1,0},{2,1},{3,2},{4,7},{5,4},{6,5},{7,6},{8,11},{9,8},{10,9... | collective-permute-start | bytes 294920 | tf_op jit(solution)/shard_map/ppermute | solution.py:540
  29.4 0.8 collective-permute-start.4
  30.2 0.7 collective-permute-start.5
  30.9 4.1 %inputs_kernel.1 = (bf16[256,768]{1,0:T(8,128)(2,1)}, bf16[256,576]{1,0:T(8,128)(2,1)}, f32[64,768]{1,0:T(8,128)}, f32[64,128]{1,0:T(8,128)}, bf16[256,768]{1,0:...) custom-call(s32[1]{0:T(128)} %bitcast.refs_0_, ...), custom_call_target="tpu_custom_call" | custom-call | flops 3000000000 | bytes 133970040 | tf_op jit(solution)/shard_map/inputs_kernel/pallas_call | solution.py:496
  35.0 0.6 collective-permute-done.4.refs_2_
  35.6 1.0 collective-permute-done.5.refs_3_
  36.6 1.7 column_out_kernel.1
  38.4 27.0 %all_to_all.25 = bf16[64,4,896]{2,1,0:T(4,128)(2,1)S(1)} all-to-all(bf16[64,4,896]{2,1,0:T(4,128)(2,1)S(1)} %reshape.38), channel_id=1, replica_groups=mesh['rows'=64,'heads'=4] {'rows'}, dimensions={0} | all-to-all | bytes 917504 | tf_op jit(solution)/shard_map/all_to_all | solution.py:549
  65.5 2.4 %column_back_kernel.1 = (bf16[256,832]{1,0:T(8,128)(2,1)S(1)}, f32[8,64]{1,0:T(8,128)S(1)}) custom-call(bf16[256,896]{1,0:T(8,128)(2,1)S(1)} %reshape.39.refs_0_), custom_call_target="tpu_custom_call" | custom-call | flops 3000000000 | bytes 26603520 | tf_op jit(solution)/shard_map/column_back_kernel/pallas_call | solution.py:496
  68.0 21.8 %all_to_all.26 = bf16[64,4,832]{2,1,0:T(4,128)(2,1)S(1)} all-to-all(bf16[64,4,832]{2,1,0:T(4,128)(2,1)S(1)} %reshape.40), channel_id=1, replica_groups=mesh['rows'=64,'heads'=4] {'rows'}, dimensions={0} | all-to-all | bytes 851968 | tf_op jit(solution)/shard_map/all_to_all | solution.py:549
  89.8 0.2 reshape.41.refs_0_.refs_2_
  90.1 0.5 column_join_kernel.1
  90.6 0.2 copy-done
  90.8 0.5 collective-permute-start.6
  91.3 2.0 collective-permute-start.7
  93.3 1.1 collective-permute-start.8
  94.5 4.8 %collective-permute-done.6.refs_2_ = bf16[64,768]{1,0:T(8,128)(2,1)S(1)} collective-permute-done((bf16[64,768]{1,0:T(8,128)(2,1)S(1)}, bf16[64,768]{1,0:T(8,128)(2,1)S(1)}, u32[]{:S(2)}, u32[]{:S(2)}) %collective-permute-start.6) | collective-permute-done | bytes 98336 | tf_op jit(solution)/shard_map/ppermute | solution.py:540
  99.3 0.6 collective-permute-done.8.refs_4_
  99.9 2.0 %residual_kernel.4 = (f32[64,768]{1,0:T(8,128)}, bf16[64,768]{1,0:T(8,128)(2,1)S(1)}) custom-call(f32[64,768]{1,0:T(8,128)} %get-tuple-element.72.refs_0_, bf16[64,768]{1,0:T(8,128)(2,1)S(1)} %get-tuple-element.84.refs_1_, bf16[64,768]{1,0:T(8,128)(2,1)S(1)} %collective-permute-done.6.refs_2_, bf16[64,768]{1,0:T(8,128)(2,1)S(1)} %collective-permute-done.7.refs_3_, ...), custom_call_target="tpu_custom_call" | custom-call | flops 3000000000 | bytes 33699840 | tf_op jit(solution)/shard_map/residual_kernel/pallas_call | solution.py:496
  101.9 1.0 collective-permute-start.10
  102.9 2.4 %collective-permute-start.11 = (bf16[64,768]{1,0:T(8,128)(2,1)S(1)}, bf16[64,768]{1,0:T(8,128)(2,1)S(1)}, u32[]{:S(2)}, u32[]{:S(2)}) collective-permute-start(bf16[64,768]{1,0:T(8,128)(2,1)S(1)} %get-tuple-element.91.refs_0_), channel_id=1, source_target_pairs={{0,1},{1,2},{2,3},{3,0},{4,5},{5,6},{6,7},{7,4},{8,9},{9,10},{10,1... | collective-permute-start | bytes 294920 | tf_op jit(solution)/shard_map/ppermute | solution.py:540
  105.3 0.9 collective-permute-start.9
  106.2 0.9 copy.26.refs_4_
  107.1 1.6 collective-permute-done.10.refs_2_
  108.6 1.0 collective-permute-done.11.refs_3_
  109.6 0.3 collective-permute-done.9.refs_1_
  110.0 2.7 %row_out_kernel.1 = (bf16[256,768]{1,0:T(8,128)(2,1)}, bf16[256,192]{1,0:T(8,128)(2,1)}, f32[64,1,192]{2,1,0:T(1,128)}) custom-call(bf16[64,768]{1,0:T(8,128)(2,1)S(1)} %get-tuple-element.91.refs_0_, bf16[64,768]{1,0:T(8,128)(2,1)S(1)} %collective-permute-done.9.refs_1_, bf16[64,768]{1,0:T(8,128)(2,1)S(1)} %collective-permute-done.10.refs_2_, ...), custom_call_target="tpu_custom_call" | custom-call | flops 3000000000 | bytes 45711360 | tf_op jit(solution)/shard_map/row_out_kernel/pallas_call | solution.py:496
  112.7 6.0 %all-to-all-start.2 = ((f32[64,1,192]{2,1,0:T(1,128)}), f32[64,1,192]{2,1,0:T(1,128)S(1)}, u32[]{:S(2)}, u32[]{:S(2)}) async-start(f32[64,1,192]{2,1,0:T(1,128)} %get-tuple-element.93), calls=%async_computation.2 | async-start | bytes 131072 | tf_op jit(solution)/shard_map/all_to_all | solution.py:549
  118.7 9.0 %all-to-all-done.2.refs_0_ = f32[64,1,192]{2,1,0:T(1,128)S(1)} async-done(((f32[64,1,192]{2,1,0:T(1,128)}), f32[64,1,192]{2,1,0:T(1,128)S(1)}, u32[]{:S(2)}, u32[]{:S(2)}) %all-to-all-start.2) | async-done | bytes 49184 | tf_op jit(solution)/shard_map/all_to_all | solution.py:549
  127.7 1.0 tied_back_kernel.1
  128.7 6.1 %all-to-all-start.3 = ((f32[64,1,192]{2,1,0:T(1,128)}), f32[64,1,192]{2,1,0:T(1,128)S(1)}, u32[]{:S(2)}, u32[]{:S(2)}) async-start(f32[64,1,192]{2,1,0:T(1,128)} %tied_back_kernel.1), calls=%async_computation.3 | async-start | bytes 131072 | tf_op jit(solution)/shard_map/all_to_all | solution.py:549
  134.9 3.9 %column_weight_kernel.1 = (bf16[32,72,128]{2,1,0:T(8,128)(2,1)}, bf16[32,72,128]{2,1,0:T(8,128)(2,1)}) custom-call(s32[2]{0:T(128)S(1)} %pad_add_fusion.refs_0_, bf16[256,768]{1,0:T(8,128)(2,1)} %get-tuple-element.110.refs_1_, bf16[256,832]{1,0:T(8,128)(2,1)} %copy-done, bf16[256,768]{1,0:T(8,128)(2,1)} %get-tuple-element.111.refs_3_), custom_call_target="tpu_custom_call" | custom-call | flops 1000 | bytes 1000 | tf_op jit(solution)/shard_map/column_weight_kernel/pallas_call | solution.py:496
  138.9 0.5 collective-permute-start.18
  139.3 2.5 %row_values_kernel.1 = (bf16[256,192]{1,0:T(8,128)(2,1)}, bf16[256,192]{1,0:T(8,128)(2,1)}) custom-call(bf16[256,832]{1,0:T(8,128)(2,1)} %copy-done, bf16[256,576]{1,0:T(8,128)(2,1)} %get-tuple-element.92.refs_5_.refs_1_.refs_3_, bf16[256,192]{1,0:T(8,128)(2,1)} %get-tuple-element.97.refs_2_), custom_call_target="tpu_custom_call" | custom-call | flops 1000 | bytes 1000 | tf_op jit(solution)/shard_map/row_values_kernel/pallas_call | solution.py:496
  141.8 2.3 %all-to-all-done.3.refs_1_ = f32[64,1,192]{2,1,0:T(1,128)S(1)} async-done(((f32[64,1,192]{2,1,0:T(1,128)}), f32[64,1,192]{2,1,0:T(1,128)S(1)}, u32[]{:S(2)}, u32[]{:S(2)}) %all-to-all-start.3) | async-done | bytes 49184 | tf_op jit(solution)/shard_map/all_to_all | solution.py:549
  144.1 3.9 %row_end_kernel.1 = (bf16[64,768]{1,0:T(8,128)(2,1)S(1)}, bf16[64,768]{1,0:T(8,128)(2,1)S(1)}, bf16[64,768]{1,0:T(8,128)(2,1)S(1)}, bf16[64,768]{1,0:T(8,128)(2,...) custom-call(s32[2]{0:T(128)S(1)} %pad_add_fusion.refs_0_, ...), custom_call_target="tpu_custom_call" | custom-call | flops 3000000000 | bytes 113541360 | tf_op jit(solution)/shard_map/row_end_kernel/pallas_call | solution.py:496
  148.0 0.2 collective-permute-start.19
  148.2 1.9 collective-permute-done.19.refs_3_
  150.1 2.4 %pair_kernel.1 = bf16[32,144,128]{2,1,0:T(8,128)(2,1)} custom-call(bf16[32,72,128]{2,1,0:T(8,128)(2,1)} %get-tuple-element.112.refs_0_, bf16[32,72,128]{2,1,0:T(8,128)(2,1)} %copy-done.4, bf16[32,72,128]{2,1,0:T(8,128)(2,1)S(1)} %get-tuple-element.115.refs_2_, bf16[32,72,128]{2,1,0:T(8,128)(2,1)S(1)} %collective-permute-done.19.refs_3_), custom_call_target="tpu_custom_call" | custom-call | flops 3000000000 | bytes 106168320 | tf_op jit(solution)/shard_map/pair_kernel/pallas_call | solution.py:496
  152.5 7.7 %all-to-all-start.4 = ((bf16[32,144,128]{2,1,0:T(8,128)(2,1)}), bf16[32,144,128]{2,1,0:T(8,128)(2,1)S(1)}, u32[]{:S(2)}, u32[]{:S(2)}) async-start(bf16[32,144,128]{2,1,0:T(8,128)(2,1)} %pair_kernel.1), calls=%async_computation.6 | async-start | bytes 2359296 | tf_op jit(solution)/shard_map/all_to_all | solution.py:549
  160.3 0.6 collective-permute-start.12
  160.9 3.5 %collective-permute-start.13 = (bf16[64,768]{1,0:T(8,128)(2,1)S(1)}, bf16[64,768]{1,0:T(8,128)(2,1)S(1)}, u32[]{:S(2)}, u32[]{:S(2)}) collective-permute-start(bf16[64,768]{1,0:T(8,128)(2,1)S(1)} %get-tuple-element.104), channel_id=1, source_target_pairs={{0,2},{1,3},{2,0},{3,1},{4,6},{5,7},{6,4},{7,5},{8,10},{9,11},{10,... | collective-permute-start | bytes 294920 | tf_op jit(solution)/shard_map/ppermute | solution.py:540
  164.4 2.4 %collective-permute-done.12.refs_2_ = bf16[64,768]{1,0:T(8,128)(2,1)S(1)} collective-permute-done((bf16[64,768]{1,0:T(8,128)(2,1)S(1)}, bf16[64,768]{1,0:T(8,128)(2,1)S(1)}, u32[]{:S(2)}, u32[]{:S(2)}) %collective-permute-start.12) | collective-permute-done | bytes 98336 | tf_op jit(solution)/shard_map/ppermute | solution.py:540
  166.7 2.2 %collective-permute-done.13.refs_3_ = bf16[64,768]{1,0:T(8,128)(2,1)S(1)} collective-permute-done((bf16[64,768]{1,0:T(8,128)(2,1)S(1)}, bf16[64,768]{1,0:T(8,128)(2,1)S(1)}, u32[]{:S(2)}, u32[]{:S(2)}) %collective-permute-start.13) | collective-permute-done | bytes 98336 | tf_op jit(solution)/shard_map/ppermute | solution.py:540
  168.9 0.2 collective-permute-done.14.refs_4_
  169.1 1.9 residual_kernel.5
  171.1 2.3 %collective-permute-start.15 = (bf16[64,768]{1,0:T(8,128)(2,1)S(1)}, bf16[64,768]{1,0:T(8,128)(2,1)S(1)}, u32[]{:S(2)}, u32[]{:S(2)}) collective-permute-start(bf16[64,768]{1,0:T(8,128)(2,1)S(1)} %get-tuple-element.108.refs_1_), channel_id=1, source_target_pairs={{0,3},{1,0},{2,1},{3,2},{4,7},{5,4},{6,5},{7,6},{8,11},{9,8},{10,9... | collective-permute-start | bytes 294920 | tf_op jit(solution)/shard_map/ppermute | solution.py:540
  173.5 0.9 collective-permute-start.17
  174.4 1.5 ffn_end_kernel.1
  175.9 1.3 collective-permute-done.15.refs_2_
  177.3 2.7 %collective-permute-done.16.refs_3_ = bf16[64,768]{1,0:T(8,128)(2,1)S(1)} collective-permute-done((bf16[64,768]{1,0:T(8,128)(2,1)S(1)}, bf16[64,768]{1,0:T(8,128)(2,1)S(1)}, u32[]{:S(2)}, u32[]{:S(2)}) %collective-permute-start.16) | collective-permute-done | bytes 98336 | tf_op jit(solution)/shard_map/ppermute | solution.py:540
  180.0 0.7 collective-permute-done.17.refs_4_
  180.7 1.0 natural_kernel.1
  181.7 9.1 %all-to-all-done.4.refs_0_ = bf16[32,144,128]{2,1,0:T(8,128)(2,1)S(1)} async-done(((bf16[32,144,128]{2,1,0:T(8,128)(2,1)}), bf16[32,144,128]{2,1,0:T(8,128)(2,1)S(1)}, u32[]{:S(2)}, u32[]{:S(2)}) %all-to-all-start.4) | async-done | bytes 1179680 | tf_op jit(solution)/shard_map/all_to_all | solution.py:549
  190.8 1.0 attention_end_kernel.1
  (27 shorter events, 0.7 us)
Async XLA Ops:
  7.2 87.3 %reduce-scatter.3.cloned.1.call-start = ((), (), s32[]{:S(2)}) async-start(), calls=%async_computation.7 | async-start | bytes 5308416 | tf_op jit(solution)/shard_map/reduce_scatter | solution.py:563
  15.8 5.8 %copy-start.1 = (bf16[768,3,192]{0,2,1:T(8,128)(2,1)S(1)}, bf16[768,3,192]{0,2,1:T(8,128)(2,1)}, u32[]{:S(2)}) copy-start(bf16[768,3,192]{0,2,1:T(8,128)(2,1)} %param.18) | copy-start | bytes 2654212
  15.9 128.2 %reduce-scatter.5.cloned.1.call-start = ((), (), s32[]{:S(2)}) async-start(), calls=%async_computation.8 | async-start | bytes 663552 | tf_op jit(solution)/shard_map/reduce_scatter | solution.py:563
  15.9 8.9 %collective-permute-start = (bf16[64,768]{1,0:T(8,128)(2,1)S(1)}, bf16[64,768]{1,0:T(8,128)(2,1)S(1)}, u32[]{:S(2)}, u32[]{:S(2)}) collective-permute-start(bf16[64,768]{1,0:T(8,128)(2,1)S(1)} %get-tuple-element.67), channel_id=1, source_target_pairs={{0,1},{1,2},{2,3},{3,0},{4,5},{5,6},{6,7},{7,4},{8,9},{9,10},{10,1... | collective-permute-start | bytes 294920 | tf_op jit(solution)/shard_map/ppermute | solution.py:540
  17.5 7.3 %collective-permute-start.1 = (bf16[64,768]{1,0:T(8,128)(2,1)S(1)}, bf16[64,768]{1,0:T(8,128)(2,1)S(1)}, u32[]{:S(2)}, u32[]{:S(2)}) collective-permute-start(bf16[64,768]{1,0:T(8,128)(2,1)S(1)} %get-tuple-element.68), channel_id=1, source_target_pairs={{0,2},{1,3},{2,0},{3,1},{4,6},{5,7},{6,4},{7,5},{8,10},{9,11},{10,... | collective-permute-start | bytes 294920 | tf_op jit(solution)/shard_map/ppermute | solution.py:540
  20.2 4.6 %collective-permute-start.2 = (bf16[64,768]{1,0:T(8,128)(2,1)S(1)}, bf16[64,768]{1,0:T(8,128)(2,1)S(1)}, u32[]{:S(2)}, u32[]{:S(2)}) collective-permute-start(bf16[64,768]{1,0:T(8,128)(2,1)S(1)} %get-tuple-element.69), channel_id=1, source_target_pairs={{0,3},{1,0},{2,1},{3,2},{4,7},{5,4},{6,5},{7,6},{8,11},{9,8},{10,9... | collective-permute-start | bytes 294920 | tf_op jit(solution)/shard_map/ppermute | solution.py:540
  22.3 1.6 copy-start.2
  26.7 8.3 %collective-permute-start.3 = (bf16[64,768]{1,0:T(8,128)(2,1)S(1)}, bf16[64,768]{1,0:T(8,128)(2,1)S(1)}, u32[]{:S(2)}, u32[]{:S(2)}) collective-permute-start(bf16[64,768]{1,0:T(8,128)(2,1)S(1)} %get-tuple-element.73.refs_0_), channel_id=1, source_target_pairs={{0,3},{1,0},{2,1},{3,2},{4,7},{5,4},{6,5},{7,6},{8,11},{9,8},{10,9... | collective-permute-start | bytes 294920 | tf_op jit(solution)/shard_map/ppermute | solution.py:540
  29.4 6.2 %collective-permute-start.4 = (bf16[64,768]{1,0:T(8,128)(2,1)S(1)}, bf16[64,768]{1,0:T(8,128)(2,1)S(1)}, u32[]{:S(2)}, u32[]{:S(2)}) collective-permute-start(bf16[64,768]{1,0:T(8,128)(2,1)S(1)} %get-tuple-element.73.refs_0_), channel_id=1, source_target_pairs={{0,2},{1,3},{2,0},{3,1},{4,6},{5,7},{6,4},{7,5},{8,10},{9,11},{10,... | collective-permute-start | bytes 294920 | tf_op jit(solution)/shard_map/ppermute | solution.py:540
  30.2 6.4 %collective-permute-start.5 = (bf16[64,768]{1,0:T(8,128)(2,1)S(1)}, bf16[64,768]{1,0:T(8,128)(2,1)S(1)}, u32[]{:S(2)}, u32[]{:S(2)}) collective-permute-start(bf16[64,768]{1,0:T(8,128)(2,1)S(1)} %get-tuple-element.73.refs_0_), channel_id=1, source_target_pairs={{0,1},{1,2},{2,3},{3,0},{4,5},{5,6},{6,7},{7,4},{8,9},{9,10},{10,1... | collective-permute-start | bytes 294920 | tf_op jit(solution)/shard_map/ppermute | solution.py:540
  90.1 0.8 copy-start
  90.8 8.4 %collective-permute-start.6 = (bf16[64,768]{1,0:T(8,128)(2,1)S(1)}, bf16[64,768]{1,0:T(8,128)(2,1)S(1)}, u32[]{:S(2)}, u32[]{:S(2)}) collective-permute-start(bf16[64,768]{1,0:T(8,128)(2,1)S(1)} %get-tuple-element.85), channel_id=1, source_target_pairs={{0,1},{1,2},{2,3},{3,0},{4,5},{5,6},{6,7},{7,4},{8,9},{9,10},{10,1... | collective-permute-start | bytes 294920 | tf_op jit(solution)/shard_map/ppermute | solution.py:540
  91.3 7.9 %collective-permute-start.7 = (bf16[64,768]{1,0:T(8,128)(2,1)S(1)}, bf16[64,768]{1,0:T(8,128)(2,1)S(1)}, u32[]{:S(2)}, u32[]{:S(2)}) collective-permute-start(bf16[64,768]{1,0:T(8,128)(2,1)S(1)} %get-tuple-element.86), channel_id=1, source_target_pairs={{0,2},{1,3},{2,0},{3,1},{4,6},{5,7},{6,4},{7,5},{8,10},{9,11},{10,... | collective-permute-start | bytes 294920 | tf_op jit(solution)/shard_map/ppermute | solution.py:540
  93.3 6.6 %collective-permute-start.8 = (bf16[64,768]{1,0:T(8,128)(2,1)S(1)}, bf16[64,768]{1,0:T(8,128)(2,1)S(1)}, u32[]{:S(2)}, u32[]{:S(2)}) collective-permute-start(bf16[64,768]{1,0:T(8,128)(2,1)S(1)} %get-tuple-element.87), channel_id=1, source_target_pairs={{0,3},{1,0},{2,1},{3,2},{4,7},{5,4},{6,5},{7,6},{8,11},{9,8},{10,9... | collective-permute-start | bytes 294920 | tf_op jit(solution)/shard_map/ppermute | solution.py:540
  99.9 6.3 %copy-start.3 = (bf16[768,192]{0,1:T(8,128)(2,1)S(1)}, bf16[768,192]{0,1:T(8,128)(2,1)}, u32[]{:S(2)}) copy-start(bf16[768,192]{0,1:T(8,128)(2,1)} %param.17) | copy-start | bytes 884740
  101.9 6.7 %collective-permute-start.10 = (bf16[64,768]{1,0:T(8,128)(2,1)S(1)}, bf16[64,768]{1,0:T(8,128)(2,1)S(1)}, u32[]{:S(2)}, u32[]{:S(2)}) collective-permute-start(bf16[64,768]{1,0:T(8,128)(2,1)S(1)} %get-tuple-element.91.refs_0_), channel_id=1, source_target_pairs={{0,2},{1,3},{2,0},{3,1},{4,6},{5,7},{6,4},{7,5},{8,10},{9,11},{10,... | collective-permute-start | bytes 294920 | tf_op jit(solution)/shard_map/ppermute | solution.py:540
  102.9 6.7 %collective-permute-start.11 = (bf16[64,768]{1,0:T(8,128)(2,1)S(1)}, bf16[64,768]{1,0:T(8,128)(2,1)S(1)}, u32[]{:S(2)}, u32[]{:S(2)}) collective-permute-start(bf16[64,768]{1,0:T(8,128)(2,1)S(1)} %get-tuple-element.91.refs_0_), channel_id=1, source_target_pairs={{0,1},{1,2},{2,3},{3,0},{4,5},{5,6},{6,7},{7,4},{8,9},{9,10},{10,1... | collective-permute-start | bytes 294920 | tf_op jit(solution)/shard_map/ppermute | solution.py:540
  105.3 4.7 %collective-permute-start.9 = (bf16[64,768]{1,0:T(8,128)(2,1)S(1)}, bf16[64,768]{1,0:T(8,128)(2,1)S(1)}, u32[]{:S(2)}, u32[]{:S(2)}) collective-permute-start(bf16[64,768]{1,0:T(8,128)(2,1)S(1)} %get-tuple-element.91.refs_0_), channel_id=1, source_target_pairs={{0,3},{1,0},{2,1},{3,2},{4,7},{5,4},{6,5},{7,6},{8,11},{9,8},{10,9... | collective-permute-start | bytes 294920 | tf_op jit(solution)/shard_map/ppermute | solution.py:540
  112.7 15.0 %all-to-all-start.2 = ((f32[64,1,192]{2,1,0:T(1,128)}), f32[64,1,192]{2,1,0:T(1,128)S(1)}, u32[]{:S(2)}, u32[]{:S(2)}) async-start(f32[64,1,192]{2,1,0:T(1,128)} %get-tuple-element.93), calls=%async_computation.2 | async-start | bytes 131072 | tf_op jit(solution)/shard_map/all_to_all | solution.py:549
  128.7 15.3 %all-to-all-start.3 = ((f32[64,1,192]{2,1,0:T(1,128)}), f32[64,1,192]{2,1,0:T(1,128)S(1)}, u32[]{:S(2)}, u32[]{:S(2)}) async-start(f32[64,1,192]{2,1,0:T(1,128)} %tied_back_kernel.1), calls=%async_computation.3 | async-start | bytes 131072 | tf_op jit(solution)/shard_map/all_to_all | solution.py:549
  138.9 9.4 %collective-permute-start.18 = (bf16[32,72,128]{2,1,0:T(8,128)(2,1)}, bf16[32,72,128]{2,1,0:T(8,128)(2,1)S(1)}, u32[]{:S(2)}, u32[]{:S(2)}) collective-permute-start(bf16[32,72,128]{2,1,0:T(8,128)(2,1)} %get-tuple-element.114), channel_id=1, source_target_pairs={{0,4},{4,0},{8,12},{12,8},{16,20},{20,16},{24,28},{28,24},{32,36},... | collective-permute-start | bytes 1769480 | tf_op jit(solution)/shard_map/ppermute | solution.py:559
  148.0 2.1 %collective-permute-start.19 = (bf16[32,72,128]{2,1,0:T(8,128)(2,1)S(1)}, bf16[32,72,128]{2,1,0:T(8,128)(2,1)S(1)}, u32[]{:S(2)}, u32[]{:S(2)}) collective-permute-start(bf16[32,72,128]{2,1,0:T(8,128)(2,1)S(1)} %get-tuple-element.116), channel_id=1, source_target_pairs={{0,4},{4,0},{8,12},{12,8},{16,20},{20,16},{24,28},{28,24},{32,36},... | collective-permute-start | bytes 1769480 | tf_op jit(solution)/shard_map/ppermute | solution.py:559
  148.2 1.9 copy-start.4
  152.5 38.2 %all-to-all-start.4 = ((bf16[32,144,128]{2,1,0:T(8,128)(2,1)}), bf16[32,144,128]{2,1,0:T(8,128)(2,1)S(1)}, u32[]{:S(2)}, u32[]{:S(2)}) async-start(bf16[32,144,128]{2,1,0:T(8,128)(2,1)} %pair_kernel.1), calls=%async_computation.6 | async-start | bytes 2359296 | tf_op jit(solution)/shard_map/all_to_all | solution.py:549
  160.3 6.5 %collective-permute-start.12 = (bf16[64,768]{1,0:T(8,128)(2,1)S(1)}, bf16[64,768]{1,0:T(8,128)(2,1)S(1)}, u32[]{:S(2)}, u32[]{:S(2)}) collective-permute-start(bf16[64,768]{1,0:T(8,128)(2,1)S(1)} %get-tuple-element.103), channel_id=1, source_target_pairs={{0,1},{1,2},{2,3},{3,0},{4,5},{5,6},{6,7},{7,4},{8,9},{9,10},{10,1... | collective-permute-start | bytes 294920 | tf_op jit(solution)/shard_map/ppermute | solution.py:540
  160.9 8.1 %collective-permute-start.13 = (bf16[64,768]{1,0:T(8,128)(2,1)S(1)}, bf16[64,768]{1,0:T(8,128)(2,1)S(1)}, u32[]{:S(2)}, u32[]{:S(2)}) collective-permute-start(bf16[64,768]{1,0:T(8,128)(2,1)S(1)} %get-tuple-element.104), channel_id=1, source_target_pairs={{0,2},{1,3},{2,0},{3,1},{4,6},{5,7},{6,4},{7,5},{8,10},{9,11},{10,... | collective-permute-start | bytes 294920 | tf_op jit(solution)/shard_map/ppermute | solution.py:540
  164.4 4.8 %collective-permute-start.14 = (bf16[64,768]{1,0:T(8,128)(2,1)S(1)}, bf16[64,768]{1,0:T(8,128)(2,1)S(1)}, u32[]{:S(2)}, u32[]{:S(2)}) collective-permute-start(bf16[64,768]{1,0:T(8,128)(2,1)S(1)} %get-tuple-element.105), channel_id=1, source_target_pairs={{0,3},{1,0},{2,1},{3,2},{4,7},{5,4},{6,5},{7,6},{8,11},{9,8},{10,9... | collective-permute-start | bytes 294920 | tf_op jit(solution)/shard_map/ppermute | solution.py:540
  171.1 6.2 %collective-permute-start.15 = (bf16[64,768]{1,0:T(8,128)(2,1)S(1)}, bf16[64,768]{1,0:T(8,128)(2,1)S(1)}, u32[]{:S(2)}, u32[]{:S(2)}) collective-permute-start(bf16[64,768]{1,0:T(8,128)(2,1)S(1)} %get-tuple-element.108.refs_1_), channel_id=1, source_target_pairs={{0,3},{1,0},{2,1},{3,2},{4,7},{5,4},{6,5},{7,6},{8,11},{9,8},{10,9... | collective-permute-start | bytes 294920 | tf_op jit(solution)/shard_map/ppermute | solution.py:540
  173.4 6.6 %collective-permute-start.16 = (bf16[64,768]{1,0:T(8,128)(2,1)S(1)}, bf16[64,768]{1,0:T(8,128)(2,1)S(1)}, u32[]{:S(2)}, u32[]{:S(2)}) collective-permute-start(bf16[64,768]{1,0:T(8,128)(2,1)S(1)} %get-tuple-element.108.refs_1_), channel_id=1, source_target_pairs={{0,2},{1,3},{2,0},{3,1},{4,6},{5,7},{6,4},{7,5},{8,10},{9,11},{10,... | collective-permute-start | bytes 294920 | tf_op jit(solution)/shard_map/ppermute | solution.py:540
  173.5 7.1 %collective-permute-start.17 = (bf16[64,768]{1,0:T(8,128)(2,1)S(1)}, bf16[64,768]{1,0:T(8,128)(2,1)S(1)}, u32[]{:S(2)}, u32[]{:S(2)}) collective-permute-start(bf16[64,768]{1,0:T(8,128)(2,1)S(1)} %get-tuple-element.108.refs_1_), channel_id=1, source_target_pairs={{0,1},{1,2},{2,3},{3,0},{4,5},{5,6},{6,7},{7,4},{8,9},{9,10},{10,1... | collective-permute-start | bytes 294920 | tf_op jit(solution)/shard_map/ppermute | solution.py:540
Sparse Core Ops, SparseCore 0:
  16.0 47.8 reduce-scatter.2
  94.6 33.8 reduce-scatter.4

commit v2 on v1

--- a/solution.py
+++ b/solution.py
@@ -612,7 +612,7 @@
             ffn_weight_kernel, [ffn_shape], n2, dpre, gop, act, small=True
         )
         gz_own, gz_narrow = call(
-            residual_kernel, [piece_full, piece], base, *parts2, xhat2, inv2, gains, near=(0, 1, 2, 3, 4), near_outs=(1,), norm=2
+            residual_kernel, [piece_full, piece], base, *parts2, xhat2, inv2, gains, near=(0, 1, 2, 3, 4), near_outs=(0, 1), norm=2
         )
         gz_parts = moves.gather_heads(gz_narrow)
         (
@@ -629,7 +629,7 @@
         gz, col_in = call(
             column_out_kernel,
             [whole, shaped(tokens, 4 * local + 2 * DH)],
-            *gz_parts, col_out, col_all, after(hi_lo, g_ffn), near=(0, 1, 2, 3), near_outs=(1,),
+            *gz_parts, col_out, col_all, after(hi_lo, g_ffn), near=(0, 1, 2, 3, 4), near_outs=(1,),
         )
         col_in = moves.messages(col_in)
         back, rprobs = call(
@@ -643,7 +643,7 @@
         )
         parts1 = moves.scatter_heads(parts1)
         gy_own, gy_narrow = call(
-            residual_kernel, [piece_full, piece], gz_own, *parts1, xhat1, inv1, gains, near=(1, 2, 3, 4), near_outs=(1,), norm=1
+            residual_kernel, [piece_full, piece], gz_own, *parts1, xhat1, inv1, gains, near=(1, 2, 3, 4), near_outs=(0, 1), norm=1
         )
         gy_parts = moves.gather_heads(gy_narrow)
         share = width // moves.rows
@@ -657,7 +657,7 @@
         gy, row_og, dprobs = call(
             row_out_kernel,
             [whole, heads_out, shaped(cols, 1, local, kind=f32)],
-            *gy_parts, row_out, row_all, near=(0, 1, 2, 3), near_outs=(2,),
+            *gy_parts, row_out, row_all, near=(0, 1, 2, 3, 4), near_outs=(1, 2),
         )
         got = moves.all_to_all(dprobs)
         col_got = moves.swap(after(col_send, dprobs))
@@ -682,7 +682,7 @@
         )
         late = moves.all_to_all(late, moves.core_groups)
         _, gx_narrow = call(
-            residual_kernel, [piece_full, piece], gy_own, *parts0, xhat0, inv0, gains, near=(1, 2, 3, 4), near_outs=(1,), norm=0
+            residual_kernel, [piece_full, piece], gy_own, *parts0, xhat0, inv0, gains, near=(1, 2, 3, 4), near_outs=(0, 1), norm=0
         )
         gx_parts = moves.gather_heads(gx_narrow)
         (input_gradient,) = call(

time: 200 us -> 200 us (level)
  transfers between devices with their start and end apart: 25 -> 25, of which waited for: 17 -> 18; matrix products, arithmetic and copies ran while one was open for 2% -> 2% of each run, Pallas kernels for 16% -> 15%
where the time goes in v2:
time: 200 us; the launch traced here: 198 us
  blocking collectives  48.8 us (24%)
  starting transfers between devices  45.3 us (23%)
  waiting for transfers between devices  43.2 us (22%)
  Pallas kernels  41.2 us (21%)
  between operations  14.4 us (7%)
  local copies, waits for them, and re-layouts  5.39 us (3%)
    all_to_all x2, blocking collectives, all_to_all(): lax.all_to_all(x, 'rows', split_axis=0, concat_axis=0, tiled=True, axis_i...  48.8 us
    pallas_call x18, Pallas kernels, call(): pl.pallas_call(kernel, out_shape=[pltpu.HBM(o.shape, o.dtype) if kind ==...  41.2 us
    ppermute x18, starting transfers between devices, shift_heads(): return lax.ppermute(x, 'heads', [(i, (i + k) % n) for i in range(n)])  25.1 us
    ppermute x18, waiting for transfers between devices, shift_heads(): return lax.ppermute(x, 'heads', [(i, (i + k) % n) for i in range(n)])  20.8 us
    all_to_all x3, waiting for transfers between devices, all_to_all(): lax.all_to_all(x, 'rows', split_axis=0, concat_axis=0, tiled=True, axis_i...  20.5 us
    all_to_all x3, starting transfers between devices, all_to_all(): lax.all_to_all(x, 'rows', split_axis=0, concat_axis=0, tiled=True, axis_i...  19.5 us
  transfers between devices with their start and end apart: 25, of which 18 were waited for; matrix products, arithmetic and copies ran while one was open for 2% of the time, Pallas kernels for 15%

profile of v2, /device:TPU:32, one launch (start us, length us, event | category | flops | bytes accessed | tf_op | source)
XLA Modules:
  0.0 198.4 jit_solution(8028103745074779932)
XLA Ops:
  7.2 4.0 %feed_forward_kernel.1 = (bf16[256,768]{1,0:T(8,128)(2,1)}, bf16[256,768]{1,0:T(8,128)(2,1)}, bf16[256,768]{1,0:T(8,128)(2,1)}, bf16[256,768]{1,0:T(8,128)(2,1)}...) custom-call(s32[1]{0:T(128)} %bitcast.refs_0_, ...), custom_call_target="tpu_custom_call" | custom-call | flops 3000000000 | bytes 163461248 | tf_op jit(solution)/shard_map/feed_forward_kernel/pallas_call | solution.py:496
  11.2 4.6 %ffn_weight_kernel.1 = f32[9216,128]{1,0:T(8,128)} custom-call(bf16[256,768]{1,0:T(8,128)(2,1)} %get-tuple-element.77.refs_0_, bf16[256,768]{1,0:T(8,128)(2,1)} %get-tuple-element.78.refs_1_, bf16[256,768]{1,0:T(8,128)(2,1)} %get-tuple-element.79.refs_2_, bf16[256,768]{1,0:T(8,128)(2,1)} %get-tuple-element.80.refs_3_), custom_call_target="tpu_custom_call" | custom-call | flops 1000 | bytes 1000 | tf_op jit(solution)/shard_map/ffn_weight_kernel/pallas_call | solution.py:496
  15.9 1.6 collective-permute-start
  17.5 2.7 %collective-permute-start.1 = (bf16[64,768]{1,0:T(8,128)(2,1)S(1)}, bf16[64,768]{1,0:T(8,128)(2,1)S(1)}, u32[]{:S(2)}, u32[]{:S(2)}) collective-permute-start(bf16[64,768]{1,0:T(8,128)(2,1)S(1)} %get-tuple-element.68), channel_id=1, source_target_pairs={{0,2},{1,3},{2,0},{3,1},{4,6},{5,7},{6,4},{7,5},{8,10},{9,11},{10,... | collective-permute-start | bytes 294920 | tf_op jit(solution)/shard_map/ppermute | solution.py:540
  20.2 1.4 collective-permute-start.2
  21.7 0.6 copy.22.refs_4_.refs_1_
  22.3 1.6 copy.23.refs_5_.refs_2_
  24.1 0.8 collective-permute-done.1.refs_3_
  24.8 1.2 residual_kernel.3
  26.0 0.7 copy-done.3
  26.7 2.6 %collective-permute-start.3 = (bf16[64,768]{1,0:T(8,128)(2,1)S(1)}, bf16[64,768]{1,0:T(8,128)(2,1)S(1)}, u32[]{:S(2)}, u32[]{:S(2)}) collective-permute-start(bf16[64,768]{1,0:T(8,128)(2,1)S(1)} %get-tuple-element.73.refs_0_), channel_id=1, source_target_pairs={{0,3},{1,0},{2,1},{3,2},{4,7},{5,4},{6,5},{7,6},{8,11},{9,8},{10,9... | collective-permute-start | bytes 294920 | tf_op jit(solution)/shard_map/ppermute | solution.py:540
  29.3 0.8 collective-permute-start.4
  30.1 0.7 collective-permute-start.5
  30.8 4.1 %inputs_kernel.1 = (bf16[256,768]{1,0:T(8,128)(2,1)}, bf16[256,576]{1,0:T(8,128)(2,1)}, f32[64,768]{1,0:T(8,128)}, f32[64,128]{1,0:T(8,128)}, bf16[256,768]{1,0:...) custom-call(s32[1]{0:T(128)} %bitcast.refs_0_, ...), custom_call_target="tpu_custom_call" | custom-call | flops 3000000000 | bytes 133970040 | tf_op jit(solution)/shard_map/inputs_kernel/pallas_call | solution.py:496
  34.9 0.6 collective-permute-done.4.refs_2_
  35.5 1.0 collective-permute-done.5.refs_3_
  36.5 1.5 column_out_kernel.1
  38.1 27.0 %all_to_all.25 = bf16[64,4,896]{2,1,0:T(4,128)(2,1)S(1)} all-to-all(bf16[64,4,896]{2,1,0:T(4,128)(2,1)S(1)} %reshape.38), channel_id=1, replica_groups=mesh['rows'=64,'heads'=4] {'rows'}, dimensions={0} | all-to-all | bytes 917504 | tf_op jit(solution)/shard_map/all_to_all | solution.py:549
  65.2 2.4 %column_back_kernel.1 = (bf16[256,832]{1,0:T(8,128)(2,1)S(1)}, f32[8,64]{1,0:T(8,128)S(1)}) custom-call(bf16[256,896]{1,0:T(8,128)(2,1)S(1)} %reshape.39.refs_0_), custom_call_target="tpu_custom_call" | custom-call | flops 3000000000 | bytes 26603520 | tf_op jit(solution)/shard_map/column_back_kernel/pallas_call | solution.py:496
  67.7 21.8 %all_to_all.26 = bf16[64,4,832]{2,1,0:T(4,128)(2,1)S(1)} all-to-all(bf16[64,4,832]{2,1,0:T(4,128)(2,1)S(1)} %reshape.40), channel_id=1, replica_groups=mesh['rows'=64,'heads'=4] {'rows'}, dimensions={0} | all-to-all | bytes 851968 | tf_op jit(solution)/shard_map/all_to_all | solution.py:549
  89.6 0.2 reshape.41.refs_0_.refs_2_
  89.8 0.5 column_join_kernel.1
  90.3 0.3 copy-done
  90.6 0.5 collective-permute-start.6
  91.1 2.0 collective-permute-start.7
  93.1 1.1 collective-permute-start.8
  94.2 4.8 %collective-permute-done.6.refs_2_ = bf16[64,768]{1,0:T(8,128)(2,1)S(1)} collective-permute-done((bf16[64,768]{1,0:T(8,128)(2,1)S(1)}, bf16[64,768]{1,0:T(8,128)(2,1)S(1)}, u32[]{:S(2)}, u32[]{:S(2)}) %collective-permute-start.6) | collective-permute-done | bytes 98336 | tf_op jit(solution)/shard_map/ppermute | solution.py:540
  99.0 0.6 collective-permute-done.8.refs_4_
  99.7 1.3 residual_kernel.4
  101.0 0.7 copy-done.2
  101.7 0.9 collective-permute-start.10
  102.6 2.4 %collective-permute-start.11 = (bf16[64,768]{1,0:T(8,128)(2,1)S(1)}, bf16[64,768]{1,0:T(8,128)(2,1)S(1)}, u32[]{:S(2)}, u32[]{:S(2)}) collective-permute-start(bf16[64,768]{1,0:T(8,128)(2,1)S(1)} %get-tuple-element.91.refs_0_), channel_id=1, source_target_pairs={{0,1},{1,2},{2,3},{3,0},{4,5},{5,6},{6,7},{7,4},{8,9},{9,10},{10,1... | collective-permute-start | bytes 294920 | tf_op jit(solution)/shard_map/ppermute | solution.py:540
  105.0 0.9 collective-permute-start.9
  106.0 2.3 %collective-permute-done.10.refs_2_ = bf16[64,768]{1,0:T(8,128)(2,1)S(1)} collective-permute-done((bf16[64,768]{1,0:T(8,128)(2,1)S(1)}, bf16[64,768]{1,0:T(8,128)(2,1)S(1)}, u32[]{:S(2)}, u32[]{:S(2)}) %collective-permute-start.10) | collective-permute-done | bytes 98336 | tf_op jit(solution)/shard_map/ppermute | solution.py:540
  108.3 1.0 collective-permute-done.11.refs_3_
  109.3 0.3 collective-permute-done.9.refs_1_
  109.7 2.4 %row_out_kernel.1 = (bf16[256,768]{1,0:T(8,128)(2,1)}, bf16[256,192]{1,0:T(8,128)(2,1)S(1)}, f32[64,1,192]{2,1,0:T(1,128)}) custom-call(bf16[64,768]{1,0:T(8,128)(2,1)S(1)} %get-tuple-element.91.refs_0_, bf16[64,768]{1,0:T(8,128)(2,1)S(1)} %collective-permute-done.9.refs_1_, bf16[64,768]{1,0:T(8,128)(2,1)S(1)} %collective-permute-done.10.refs_2_, ...), custom_call_target="tpu_custom_call" | custom-call | flops 3000000000 | bytes 45711360 | tf_op jit(solution)/shard_map/row_out_kernel/pallas_call | solution.py:496
  112.0 0.6 copy-done.1
  112.7 6.0 %all-to-all-start.2 = ((f32[64,1,192]{2,1,0:T(1,128)}), f32[64,1,192]{2,1,0:T(1,128)S(1)}, u32[]{:S(2)}, u32[]{:S(2)}) async-start(f32[64,1,192]{2,1,0:T(1,128)} %get-tuple-element.93), calls=%async_computation.2 | async-start | bytes 131072 | tf_op jit(solution)/shard_map/all_to_all | solution.py:549
  118.7 9.2 %all-to-all-done.2.refs_0_ = f32[64,1,192]{2,1,0:T(1,128)S(1)} async-done(((f32[64,1,192]{2,1,0:T(1,128)}), f32[64,1,192]{2,1,0:T(1,128)S(1)}, u32[]{:S(2)}, u32[]{:S(2)}) %all-to-all-start.2) | async-done | bytes 49184 | tf_op jit(solution)/shard_map/all_to_all | solution.py:549
  127.9 1.0 tied_back_kernel.1
  128.9 5.8 %all-to-all-start.3 = ((f32[64,1,192]{2,1,0:T(1,128)}), f32[64,1,192]{2,1,0:T(1,128)S(1)}, u32[]{:S(2)}, u32[]{:S(2)}) async-start(f32[64,1,192]{2,1,0:T(1,128)} %tied_back_kernel.1), calls=%async_computation.3 | async-start | bytes 131072 | tf_op jit(solution)/shard_map/all_to_all | solution.py:549
  134.7 3.9 %column_weight_kernel.1 = (bf16[32,72,128]{2,1,0:T(8,128)(2,1)}, bf16[32,72,128]{2,1,0:T(8,128)(2,1)}) custom-call(s32[2]{0:T(128)S(1)} %pad_add_fusion.refs_0_, bf16[256,768]{1,0:T(8,128)(2,1)} %get-tuple-element.110.refs_1_, bf16[256,832]{1,0:T(8,128)(2,1)} %copy-done, bf16[256,768]{1,0:T(8,128)(2,1)} %get-tuple-element.111.refs_3_), custom_call_target="tpu_custom_call" | custom-call | flops 1000 | bytes 1000 | tf_op jit(solution)/shard_map/column_weight_kernel/pallas_call | solution.py:496
  138.7 0.5 collective-permute-start.18
  139.1 2.4 %row_values_kernel.1 = (bf16[256,192]{1,0:T(8,128)(2,1)}, bf16[256,192]{1,0:T(8,128)(2,1)}) custom-call(bf16[256,832]{1,0:T(8,128)(2,1)} %copy-done, bf16[256,576]{1,0:T(8,128)(2,1)} %get-tuple-element.92.refs_5_.refs_1_.refs_3_, bf16[256,192]{1,0:T(8,128)(2,1)} %copy-done.1), custom_call_target="tpu_custom_call" | custom-call | flops 1000 | bytes 1000 | tf_op jit(solution)/shard_map/row_values_kernel/pallas_call | solution.py:496
  141.6 2.3 %all-to-all-done.3.refs_1_ = f32[64,1,192]{2,1,0:T(1,128)S(1)} async-done(((f32[64,1,192]{2,1,0:T(1,128)}), f32[64,1,192]{2,1,0:T(1,128)S(1)}, u32[]{:S(2)}, u32[]{:S(2)}) %all-to-all-start.3) | async-done | bytes 49184 | tf_op jit(solution)/shard_map/all_to_all | solution.py:549
  143.9 3.9 %row_end_kernel.1 = (bf16[64,768]{1,0:T(8,128)(2,1)S(1)}, bf16[64,768]{1,0:T(8,128)(2,1)S(1)}, bf16[64,768]{1,0:T(8,128)(2,1)S(1)}, bf16[64,768]{1,0:T(8,128)(2,...) custom-call(s32[2]{0:T(128)S(1)} %pad_add_fusion.refs_0_, ...), custom_call_target="tpu_custom_call" | custom-call | flops 3000000000 | bytes 113541360 | tf_op jit(solution)/shard_map/row_end_kernel/pallas_call | solution.py:496
  148.0 1.9 collective-permute-done.19.refs_3_
  149.9 2.4 %pair_kernel.1 = bf16[32,144,128]{2,1,0:T(8,128)(2,1)} custom-call(bf16[32,72,128]{2,1,0:T(8,128)(2,1)} %get-tuple-element.112.refs_0_, bf16[32,72,128]{2,1,0:T(8,128)(2,1)} %copy-done.7, bf16[32,72,128]{2,1,0:T(8,128)(2,1)S(1)} %get-tuple-element.115.refs_2_, bf16[32,72,128]{2,1,0:T(8,128)(2,1)S(1)} %collective-permute-done.19.refs_3_), custom_call_target="tpu_custom_call" | custom-call | flops 3000000000 | bytes 106168320 | tf_op jit(solution)/shard_map/pair_kernel/pallas_call | solution.py:496
  152.3 7.7 %all-to-all-start.4 = ((bf16[32,144,128]{2,1,0:T(8,128)(2,1)}), bf16[32,144,128]{2,1,0:T(8,128)(2,1)S(1)}, u32[]{:S(2)}, u32[]{:S(2)}) async-start(bf16[32,144,128]{2,1,0:T(8,128)(2,1)} %pair_kernel.1), calls=%async_computation.6 | async-start | bytes 2359296 | tf_op jit(solution)/shard_map/all_to_all | solution.py:549
  160.1 0.8 collective-permute-start.12
  160.8 3.4 %collective-permute-start.13 = (bf16[64,768]{1,0:T(8,128)(2,1)S(1)}, bf16[64,768]{1,0:T(8,128)(2,1)S(1)}, u32[]{:S(2)}, u32[]{:S(2)}) collective-permute-start(bf16[64,768]{1,0:T(8,128)(2,1)S(1)} %get-tuple-element.104), channel_id=1, source_target_pairs={{0,2},{1,3},{2,0},{3,1},{4,6},{5,7},{6,4},{7,5},{8,10},{9,11},{10,... | collective-permute-start | bytes 294920 | tf_op jit(solution)/shard_map/ppermute | solution.py:540
  164.3 2.1 %collective-permute-done.12.refs_2_ = bf16[64,768]{1,0:T(8,128)(2,1)S(1)} collective-permute-done((bf16[64,768]{1,0:T(8,128)(2,1)S(1)}, bf16[64,768]{1,0:T(8,128)(2,1)S(1)}, u32[]{:S(2)}, u32[]{:S(2)}) %collective-permute-start.12) | collective-permute-done | bytes 98336 | tf_op jit(solution)/shard_map/ppermute | solution.py:540
  166.4 2.4 %collective-permute-done.13.refs_3_ = bf16[64,768]{1,0:T(8,128)(2,1)S(1)} collective-permute-done((bf16[64,768]{1,0:T(8,128)(2,1)S(1)}, bf16[64,768]{1,0:T(8,128)(2,1)S(1)}, u32[]{:S(2)}, u32[]{:S(2)}) %collective-permute-start.13) | collective-permute-done | bytes 98336 | tf_op jit(solution)/shard_map/ppermute | solution.py:540
  168.9 1.9 residual_kernel.5
  170.9 2.3 %collective-permute-start.15 = (bf16[64,768]{1,0:T(8,128)(2,1)S(1)}, bf16[64,768]{1,0:T(8,128)(2,1)S(1)}, u32[]{:S(2)}, u32[]{:S(2)}) collective-permute-start(bf16[64,768]{1,0:T(8,128)(2,1)S(1)} %get-tuple-element.108.refs_1_), channel_id=1, source_target_pairs={{0,3},{1,0},{2,1},{3,2},{4,7},{5,4},{6,5},{7,6},{8,11},{9,8},{10,9... | collective-permute-start | bytes 294920 | tf_op jit(solution)/shard_map/ppermute | solution.py:540
  173.3 0.9 collective-permute-start.17
  174.2 1.5 ffn_end_kernel.1
  175.7 1.3 collective-permute-done.15.refs_2_
  177.1 2.7 %collective-permute-done.16.refs_3_ = bf16[64,768]{1,0:T(8,128)(2,1)S(1)} collective-permute-done((bf16[64,768]{1,0:T(8,128)(2,1)S(1)}, bf16[64,768]{1,0:T(8,128)(2,1)S(1)}, u32[]{:S(2)}, u32[]{:S(2)}) %collective-permute-start.16) | collective-permute-done | bytes 98336 | tf_op jit(solution)/shard_map/ppermute | solution.py:540
  179.8 0.7 collective-permute-done.17.refs_4_
  180.4 1.0 natural_kernel.1
  181.5 9.1 %all-to-all-done.4.refs_0_ = bf16[32,144,128]{2,1,0:T(8,128)(2,1)S(1)} async-done(((bf16[32,144,128]{2,1,0:T(8,128)(2,1)}), bf16[32,144,128]{2,1,0:T(8,128)(2,1)S(1)}, u32[]{:S(2)}, u32[]{:S(2)}) %all-to-all-start.4) | async-done | bytes 1179680 | tf_op jit(solution)/shard_map/all_to_all | solution.py:549
  190.6 1.0 attention_end_kernel.1
  (33 shorter events, 1.3 us)
Async XLA Ops:
  7.2 87.0 %reduce-scatter.3.cloned.1.call-start = ((), (), s32[]{:S(2)}) async-start(), calls=%async_computation.7 | async-start | bytes 5308416 | tf_op jit(solution)/shard_map/reduce_scatter | solution.py:563
  15.8 5.8 %copy-start.4 = (bf16[768,3,192]{0,2,1:T(8,128)(2,1)S(1)}, bf16[768,3,192]{0,2,1:T(8,128)(2,1)}, u32[]{:S(2)}) copy-start(bf16[768,3,192]{0,2,1:T(8,128)(2,1)} %param.18) | copy-start | bytes 2654212
  15.9 128.0 %reduce-scatter.5.cloned.1.call-start = ((), (), s32[]{:S(2)}) async-start(), calls=%async_computation.8 | async-start | bytes 663552 | tf_op jit(solution)/shard_map/reduce_scatter | solution.py:563
  15.9 8.2 %collective-permute-start = (bf16[64,768]{1,0:T(8,128)(2,1)S(1)}, bf16[64,768]{1,0:T(8,128)(2,1)S(1)}, u32[]{:S(2)}, u32[]{:S(2)}) collective-permute-start(bf16[64,768]{1,0:T(8,128)(2,1)S(1)} %get-tuple-element.67), channel_id=1, source_target_pairs={{0,1},{1,2},{2,3},{3,0},{4,5},{5,6},{6,7},{7,4},{8,9},{9,10},{10,1... | collective-permute-start | bytes 294920 | tf_op jit(solution)/shard_map/ppermute | solution.py:540
  17.5 7.3 %collective-permute-start.1 = (bf16[64,768]{1,0:T(8,128)(2,1)S(1)}, bf16[64,768]{1,0:T(8,128)(2,1)S(1)}, u32[]{:S(2)}, u32[]{:S(2)}) collective-permute-start(bf16[64,768]{1,0:T(8,128)(2,1)S(1)} %get-tuple-element.68), channel_id=1, source_target_pairs={{0,2},{1,3},{2,0},{3,1},{4,6},{5,7},{6,4},{7,5},{8,10},{9,11},{10,... | collective-permute-start | bytes 294920 | tf_op jit(solution)/shard_map/ppermute | solution.py:540
  20.2 4.6 %collective-permute-start.2 = (bf16[64,768]{1,0:T(8,128)(2,1)S(1)}, bf16[64,768]{1,0:T(8,128)(2,1)S(1)}, u32[]{:S(2)}, u32[]{:S(2)}) collective-permute-start(bf16[64,768]{1,0:T(8,128)(2,1)S(1)} %get-tuple-element.69), channel_id=1, source_target_pairs={{0,3},{1,0},{2,1},{3,2},{4,7},{5,4},{6,5},{7,6},{8,11},{9,8},{10,9... | collective-permute-start | bytes 294920 | tf_op jit(solution)/shard_map/ppermute | solution.py:540
  22.3 1.6 copy-start.5
  26.0 0.7 copy-start.3
  26.7 8.2 %collective-permute-start.3 = (bf16[64,768]{1,0:T(8,128)(2,1)S(1)}, bf16[64,768]{1,0:T(8,128)(2,1)S(1)}, u32[]{:S(2)}, u32[]{:S(2)}) collective-permute-start(bf16[64,768]{1,0:T(8,128)(2,1)S(1)} %get-tuple-element.73.refs_0_), channel_id=1, source_target_pairs={{0,3},{1,0},{2,1},{3,2},{4,7},{5,4},{6,5},{7,6},{8,11},{9,8},{10,9... | collective-permute-start | bytes 294920 | tf_op jit(solution)/shard_map/ppermute | solution.py:540
  29.3 6.2 %collective-permute-start.4 = (bf16[64,768]{1,0:T(8,128)(2,1)S(1)}, bf16[64,768]{1,0:T(8,128)(2,1)S(1)}, u32[]{:S(2)}, u32[]{:S(2)}) collective-permute-start(bf16[64,768]{1,0:T(8,128)(2,1)S(1)} %get-tuple-element.73.refs_0_), channel_id=1, source_target_pairs={{0,2},{1,3},{2,0},{3,1},{4,6},{5,7},{6,4},{7,5},{8,10},{9,11},{10,... | collective-permute-start | bytes 294920 | tf_op jit(solution)/shard_map/ppermute | solution.py:540
  30.1 6.4 %collective-permute-start.5 = (bf16[64,768]{1,0:T(8,128)(2,1)S(1)}, bf16[64,768]{1,0:T(8,128)(2,1)S(1)}, u32[]{:S(2)}, u32[]{:S(2)}) collective-permute-start(bf16[64,768]{1,0:T(8,128)(2,1)S(1)} %get-tuple-element.73.refs_0_), channel_id=1, source_target_pairs={{0,1},{1,2},{2,3},{3,0},{4,5},{5,6},{6,7},{7,4},{8,9},{9,10},{10,1... | collective-permute-start | bytes 294920 | tf_op jit(solution)/shard_map/ppermute | solution.py:540
  89.8 0.8 copy-start
  90.6 8.4 %collective-permute-start.6 = (bf16[64,768]{1,0:T(8,128)(2,1)S(1)}, bf16[64,768]{1,0:T(8,128)(2,1)S(1)}, u32[]{:S(2)}, u32[]{:S(2)}) collective-permute-start(bf16[64,768]{1,0:T(8,128)(2,1)S(1)} %get-tuple-element.85), channel_id=1, source_target_pairs={{0,1},{1,2},{2,3},{3,0},{4,5},{5,6},{6,7},{7,4},{8,9},{9,10},{10,1... | collective-permute-start | bytes 294920 | tf_op jit(solution)/shard_map/ppermute | solution.py:540
  91.1 7.9 %collective-permute-start.7 = (bf16[64,768]{1,0:T(8,128)(2,1)S(1)}, bf16[64,768]{1,0:T(8,128)(2,1)S(1)}, u32[]{:S(2)}, u32[]{:S(2)}) collective-permute-start(bf16[64,768]{1,0:T(8,128)(2,1)S(1)} %get-tuple-element.86), channel_id=1, source_target_pairs={{0,2},{1,3},{2,0},{3,1},{4,6},{5,7},{6,4},{7,5},{8,10},{9,11},{10,... | collective-permute-start | bytes 294920 | tf_op jit(solution)/shard_map/ppermute | solution.py:540
  93.1 6.6 %collective-permute-start.8 = (bf16[64,768]{1,0:T(8,128)(2,1)S(1)}, bf16[64,768]{1,0:T(8,128)(2,1)S(1)}, u32[]{:S(2)}, u32[]{:S(2)}) collective-permute-start(bf16[64,768]{1,0:T(8,128)(2,1)S(1)} %get-tuple-element.87), channel_id=1, source_target_pairs={{0,3},{1,0},{2,1},{3,2},{4,7},{5,4},{6,5},{7,6},{8,11},{9,8},{10,9... | collective-permute-start | bytes 294920 | tf_op jit(solution)/shard_map/ppermute | solution.py:540
  99.7 6.2 %copy-start.6 = (bf16[768,192]{0,1:T(8,128)(2,1)S(1)}, bf16[768,192]{0,1:T(8,128)(2,1)}, u32[]{:S(2)}) copy-start(bf16[768,192]{0,1:T(8,128)(2,1)} %param.17) | copy-start | bytes 884740
  101.0 0.7 copy-start.2
  101.7 6.6 %collective-permute-start.10 = (bf16[64,768]{1,0:T(8,128)(2,1)S(1)}, bf16[64,768]{1,0:T(8,128)(2,1)S(1)}, u32[]{:S(2)}, u32[]{:S(2)}) collective-permute-start(bf16[64,768]{1,0:T(8,128)(2,1)S(1)} %get-tuple-element.91.refs_0_), channel_id=1, source_target_pairs={{0,2},{1,3},{2,0},{3,1},{4,6},{5,7},{6,4},{7,5},{8,10},{9,11},{10,... | collective-permute-start | bytes 294920 | tf_op jit(solution)/shard_map/ppermute | solution.py:540
  102.6 6.7 %collective-permute-start.11 = (bf16[64,768]{1,0:T(8,128)(2,1)S(1)}, bf16[64,768]{1,0:T(8,128)(2,1)S(1)}, u32[]{:S(2)}, u32[]{:S(2)}) collective-permute-start(bf16[64,768]{1,0:T(8,128)(2,1)S(1)} %get-tuple-element.91.refs_0_), channel_id=1, source_target_pairs={{0,1},{1,2},{2,3},{3,0},{4,5},{5,6},{6,7},{7,4},{8,9},{9,10},{10,1... | collective-permute-start | bytes 294920 | tf_op jit(solution)/shard_map/ppermute | solution.py:540
  105.0 4.7 %collective-permute-start.9 = (bf16[64,768]{1,0:T(8,128)(2,1)S(1)}, bf16[64,768]{1,0:T(8,128)(2,1)S(1)}, u32[]{:S(2)}, u32[]{:S(2)}) collective-permute-start(bf16[64,768]{1,0:T(8,128)(2,1)S(1)} %get-tuple-element.91.refs_0_), channel_id=1, source_target_pairs={{0,3},{1,0},{2,1},{3,2},{4,7},{5,4},{6,5},{7,6},{8,11},{9,8},{10,9... | collective-permute-start | bytes 294920 | tf_op jit(solution)/shard_map/ppermute | solution.py:540
  112.0 0.6 copy-start.1
  112.7 15.2 %all-to-all-start.2 = ((f32[64,1,192]{2,1,0:T(1,128)}), f32[64,1,192]{2,1,0:T(1,128)S(1)}, u32[]{:S(2)}, u32[]{:S(2)}) async-start(f32[64,1,192]{2,1,0:T(1,128)} %get-tuple-element.93), calls=%async_computation.2 | async-start | bytes 131072 | tf_op jit(solution)/shard_map/all_to_all | solution.py:549
  128.9 15.0 %all-to-all-start.3 = ((f32[64,1,192]{2,1,0:T(1,128)}), f32[64,1,192]{2,1,0:T(1,128)S(1)}, u32[]{:S(2)}, u32[]{:S(2)}) async-start(f32[64,1,192]{2,1,0:T(1,128)} %tied_back_kernel.1), calls=%async_computation.3 | async-start | bytes 131072 | tf_op jit(solution)/shard_map/all_to_all | solution.py:549
  138.7 9.4 %collective-permute-start.18 = (bf16[32,72,128]{2,1,0:T(8,128)(2,1)}, bf16[32,72,128]{2,1,0:T(8,128)(2,1)S(1)}, u32[]{:S(2)}, u32[]{:S(2)}) collective-permute-start(bf16[32,72,128]{2,1,0:T(8,128)(2,1)} %get-tuple-element.114), channel_id=1, source_target_pairs={{0,4},{4,0},{8,12},{12,8},{16,20},{20,16},{24,28},{28,24},{32,36},... | collective-permute-start | bytes 1769480 | tf_op jit(solution)/shard_map/ppermute | solution.py:559
  147.8 2.1 %collective-permute-start.19 = (bf16[32,72,128]{2,1,0:T(8,128)(2,1)S(1)}, bf16[32,72,128]{2,1,0:T(8,128)(2,1)S(1)}, u32[]{:S(2)}, u32[]{:S(2)}) collective-permute-start(bf16[32,72,128]{2,1,0:T(8,128)(2,1)S(1)} %get-tuple-element.116), channel_id=1, source_target_pairs={{0,4},{4,0},{8,12},{12,8},{16,20},{20,16},{24,28},{28,24},{32,36},... | collective-permute-start | bytes 1769480 | tf_op jit(solution)/shard_map/ppermute | solution.py:559
  148.0 1.9 copy-start.7
  152.3 38.2 %all-to-all-start.4 = ((bf16[32,144,128]{2,1,0:T(8,128)(2,1)}), bf16[32,144,128]{2,1,0:T(8,128)(2,1)S(1)}, u32[]{:S(2)}, u32[]{:S(2)}) async-start(bf16[32,144,128]{2,1,0:T(8,128)(2,1)} %pair_kernel.1), calls=%async_computation.6 | async-start | bytes 2359296 | tf_op jit(solution)/shard_map/all_to_all | solution.py:549
  160.1 6.3 %collective-permute-start.12 = (bf16[64,768]{1,0:T(8,128)(2,1)S(1)}, bf16[64,768]{1,0:T(8,128)(2,1)S(1)}, u32[]{:S(2)}, u32[]{:S(2)}) collective-permute-start(bf16[64,768]{1,0:T(8,128)(2,1)S(1)} %get-tuple-element.103), channel_id=1, source_target_pairs={{0,1},{1,2},{2,3},{3,0},{4,5},{5,6},{6,7},{7,4},{8,9},{9,10},{10,1... | collective-permute-start | bytes 294920 | tf_op jit(solution)/shard_map/ppermute | solution.py:540
  160.8 8.0 %collective-permute-start.13 = (bf16[64,768]{1,0:T(8,128)(2,1)S(1)}, bf16[64,768]{1,0:T(8,128)(2,1)S(1)}, u32[]{:S(2)}, u32[]{:S(2)}) collective-permute-start(bf16[64,768]{1,0:T(8,128)(2,1)S(1)} %get-tuple-element.104), channel_id=1, source_target_pairs={{0,2},{1,3},{2,0},{3,1},{4,6},{5,7},{6,4},{7,5},{8,10},{9,11},{10,... | collective-permute-start | bytes 294920 | tf_op jit(solution)/shard_map/ppermute | solution.py:540
  164.3 4.7 %collective-permute-start.14 = (bf16[64,768]{1,0:T(8,128)(2,1)S(1)}, bf16[64,768]{1,0:T(8,128)(2,1)S(1)}, u32[]{:S(2)}, u32[]{:S(2)}) collective-permute-start(bf16[64,768]{1,0:T(8,128)(2,1)S(1)} %get-tuple-element.105), channel_id=1, source_target_pairs={{0,3},{1,0},{2,1},{3,2},{4,7},{5,4},{6,5},{7,6},{8,11},{9,8},{10,9... | collective-permute-start | bytes 294920 | tf_op jit(solution)/shard_map/ppermute | solution.py:540
  170.9 6.2 %collective-permute-start.15 = (bf16[64,768]{1,0:T(8,128)(2,1)S(1)}, bf16[64,768]{1,0:T(8,128)(2,1)S(1)}, u32[]{:S(2)}, u32[]{:S(2)}) collective-permute-start(bf16[64,768]{1,0:T(8,128)(2,1)S(1)} %get-tuple-element.108.refs_1_), channel_id=1, source_target_pairs={{0,3},{1,0},{2,1},{3,2},{4,7},{5,4},{6,5},{7,6},{8,11},{9,8},{10,9... | collective-permute-start | bytes 294920 | tf_op jit(solution)/shard_map/ppermute | solution.py:540
  173.2 6.6 %collective-permute-start.16 = (bf16[64,768]{1,0:T(8,128)(2,1)S(1)}, bf16[64,768]{1,0:T(8,128)(2,1)S(1)}, u32[]{:S(2)}, u32[]{:S(2)}) collective-permute-start(bf16[64,768]{1,0:T(8,128)(2,1)S(1)} %get-tuple-element.108.refs_1_), channel_id=1, source_target_pairs={{0,2},{1,3},{2,0},{3,1},{4,6},{5,7},{6,4},{7,5},{8,10},{9,11},{10,... | collective-permute-start | bytes 294920 | tf_op jit(solution)/shard_map/ppermute | solution.py:540
  173.3 7.1 %collective-permute-start.17 = (bf16[64,768]{1,0:T(8,128)(2,1)S(1)}, bf16[64,768]{1,0:T(8,128)(2,1)S(1)}, u32[]{:S(2)}, u32[]{:S(2)}) collective-permute-start(bf16[64,768]{1,0:T(8,128)(2,1)S(1)} %get-tuple-element.108.refs_1_), channel_id=1, source_target_pairs={{0,1},{1,2},{2,3},{3,0},{4,5},{5,6},{6,7},{7,4},{8,9},{9,10},{10,1... | collective-permute-start | bytes 294920 | tf_op jit(solution)/shard_map/ppermute | solution.py:540
Sparse Core Ops, SparseCore 0:
  16.0 48.0 reduce-scatter.2
  94.3 33.9 reduce-scatter.4
